TPU v7x, 512 devices: a whole 4x8x8 slice. The times are simulated.
512 devices in a mesh: blk: 64 (over y, z_lo, core), row: 8 (over z_hi, x).
Axes of the slice: x: 4, y: 8, z: 8 (z_hi: 2, z_lo: 4; z = z_hi * 4 + z_lo), core: 2. Of those that a mesh axis runs over, the one named last changes fastest.
Arguments:
- features: float32 [32, 393216], P(None, ('blk', 'row')), may hold values from -6 to 6
- probes: bfloat16 [8, 393216], P(None, ('blk', 'row')), may hold values from -5 to 5
- inverse_scales: float32 [32], replicated, may hold values from 0.02 to 0.2
- round_index: int32 [1], replicated, may hold values from 1 to 31
- pivots: int32 [128], replicated, may hold values from 0 to 393215
Outputs:
- product: float32 [8, 393216], P(None, ('blk', 'row'))
- projection: float32 [8, 128], replicated
- quadratic: float32 [8], replicated
Inputs may be any that keep to these rules, and one draw needn't show every extreme that they name: `pivots`: indices may repeat.
All inputs are finite; a program needn't handle non-finite values.
Results may differ from a plain program's by a relative error of at most 0.034.
Values may be sent and summed in bfloat16 or wider, within the bound.
No kernel may reach another device: no remote copies, remote signals or barrier semaphores. Data moves between devices by JAX's collectives and lax.ppermute only.
A program may use at most 64 MiB of HBM per device.

v0:
```python
import math

import jax
import jax.numpy as jnp
from jax import lax
from jax.sharding import PartitionSpec as P


def passed_along(x, axis, by):
    peers = lax.axis_size(axis)
    return lax.ppermute(x, axis, [(i, (i + by) % peers) for i in range(peers)])


def square_norm(scaled_feat):
    wide = scaled_feat.astype(jnp.float32)
    return jnp.sum(wide * wide, axis=0)


def kernel_block(row_feat, row_norm, col_feat, col_norm):
    inner_prod = jnp.dot(row_feat.T, col_feat, preferred_element_type=jnp.float32)
    distance = row_norm[:, None] + col_norm[None, :] - 2.0 * inner_prod
    return jnp.exp(-0.5 * distance).astype(jnp.bfloat16)


def body(features, probes, inverse_scales, round_index, pivots):
    feat_count = features.shape[0]
    row_count = features.shape[1]
    probe_count = probes.shape[0]
    group_count = lax.axis_size("blk")
    row_devices = lax.axis_size("row")
    group_index = lax.axis_index("blk")
    row_index = lax.axis_index("row")
    block_points = row_count * row_devices
    total_points = block_points * group_count
    round_shift = round_index[0]
    bit_count = group_count.bit_length() - 1
    scaled = (features * jnp.sqrt(inverse_scales)[:, None]).astype(jnp.bfloat16)
    own_norm = square_norm(scaled)
    global_rows = (group_index * row_devices + row_index) * row_count + jnp.arange(
        row_count, dtype=jnp.int32
    )
    pivot_mask = (global_rows[:, None] == pivots[None, :]).astype(jnp.bfloat16)
    pivot_part = jnp.dot(scaled, pivot_mask, preferred_element_type=jnp.float32)
    pivot_feat = lax.psum(pivot_part, ("blk", "row")).astype(jnp.bfloat16)
    pivot_norm = square_norm(pivot_feat)
    pivot_kernel = kernel_block(scaled, own_norm, pivot_feat, pivot_norm)
    projection_part = jnp.dot(probes, pivot_kernel, preferred_element_type=jnp.float32)
    projection_scale = 8.0 / math.sqrt(total_points)
    projection = lax.psum(projection_part, ("blk", "row")) * projection_scale
    packed = jnp.concatenate([scaled, probes], axis=0)
    partner_data = packed
    for bit_number in range(bit_count):
        stepped = passed_along(partner_data, "blk", -(1 << bit_number))
        partner_data = jnp.where(round_shift >> bit_number & 1 == 1, stepped, partner_data)
    shard_piece = lax.all_gather(partner_data, "row", axis=1, tiled=True)
    forward = jnp.zeros((probe_count, row_count), jnp.float32)
    backward = jnp.zeros((probe_count, block_points), jnp.float32)
    col_count = shard_piece.shape[1]
    block_cols = math.gcd(col_count, 2048)
    for offset in range(0, col_count, block_cols):
        col_part = shard_piece[:, offset : offset + block_cols]
        col_feat = col_part[:feat_count]
        col_probe = col_part[feat_count:]
        kernel = kernel_block(scaled, own_norm, col_feat, square_norm(col_feat))
        forward = forward + lax.dot_general(
            col_probe, kernel, (((1,), (1,)), ((), ())), preferred_element_type=jnp.float32
        )
        back_part = jnp.dot(probes, kernel, preferred_element_type=jnp.float32)
        backward = lax.dynamic_update_slice_in_dim(backward, back_part, offset, 1)
    forward, backward = (forward, backward)
    summed = lax.psum(backward, "row")
    back_share = lax.dynamic_slice_in_dim(summed, row_index * row_count, row_count, 1)
    for bit_number in range(bit_count):
        stepped_back = passed_along(back_share, "blk", 1 << bit_number)
        back_share = jnp.where(round_shift >> bit_number & 1 == 1, stepped_back, back_share)
    product = 8.0 / math.sqrt(block_points) * (forward + back_share)
    quadratic_part = jnp.sum(probes.astype(jnp.float32) * product, axis=1)
    quadratic = lax.psum(quadratic_part, ("blk", "row")) / math.sqrt(total_points)
    return (product, projection, quadratic)


def solution(mesh):
    return jax.shard_map(
        body,
        mesh=mesh,
        in_specs=(P(None, ("blk", "row")), P(None, ("blk", "row")), P(), P(), P()),
        out_specs=(P(None, ("blk", "row")), P(), P()),
        check_vma=False,
    )
```

profile of v0, /device:TPU:1, one launch (start us, length us, event | category | flops | bytes accessed | tf_op | source)
XLA Modules:
  0.0 475.4 jit_solution(17229605950394066575)
XLA Ops:
  9.6 8.8 %collective-permute-start = (bf16[40,768]{1,0:T(8,128)(2,1)S(1)}, bf16[40,768]{1,0:T(8,128)(2,1)S(1)}, u32[]{:S(2)}, u32[]{:S(2)}) collective-permute-start(bf16[40,768]{1,0:T(8,128)(2,1)S(1)} %pad_maximum_fusion), channel_id=1, source_target_pairs={{0,504},{8,0},{16,8},{24,16},{32,24},{40,32},{48,40},{56,48},{64,5... | collective-permute-start | bytes 184328 | tf_op jit(solution)/shard_map/ppermute | solution.py:11
  20.0 11.1 %collective-permute-start.1 = (bf16[40,768]{1,0:T(8,128)(2,1)S(1)}, bf16[40,768]{1,0:T(8,128)(2,1)S(1)}, u32[]{:S(2)}, u32[]{:S(2)}) collective-permute-start(bf16[40,768]{1,0:T(8,128)(2,1)S(1)} %broadcast_select_fusion), channel_id=1, source_target_pairs={{0,496},{8,504},{16,0},{24,8},{32,16},{40,24},{48,32},{56,40},{64,... | collective-permute-start | bytes 184328 | tf_op jit(solution)/shard_map/ppermute | solution.py:11
  31.1 1.3 collective-permute-done.1
  32.4 2.5 collective-permute-start.2
  34.9 3.3 collective-permute-done.2
  38.3 2.4 collective-permute-start.3
  40.7 3.1 collective-permute-done.3
  43.8 2.2 collective-permute-start.4
  46.0 4.7 collective-permute-done.4
  50.7 4.3 collective-permute-start.5
  55.0 5.3 %collective-permute-done.5 = bf16[40,768]{1,0:T(8,128)(2,1)S(1)} collective-permute-done((bf16[40,768]{1,0:T(8,128)(2,1)S(1)}, bf16[40,768]{1,0:T(8,128)(2,1)S(1)}, u32[]{:S(2)}, u32[]{:S(2)}) %collective-permute-start.5) | collective-permute-done | bytes 61472 | tf_op jit(solution)/shard_map/ppermute | solution.py:11
  60.3 40.2 %all_gather.3 = bf16[40,6144]{1,0:T(8,128)(2,1)S(1)} all-gather(bf16[40,768]{1,0:T(8,128)(2,1)S(1)} %broadcast_select_fusion.5), channel_id=1, replica_groups=mesh['blk'=64,'row'=8] {'row'}, dimensions={1}, use_global_device_ids=true | all-gather | bytes 552960 | tf_op jit(solution)/shard_map/all_gather | solution.py:55
  100.6 1.6 exponential_convert_fusion.2
  102.7 1.6 exponential_convert_fusion
  104.3 1.6 exponential_convert_fusion.1
  105.9 1.6 copy-done
  109.3 114.5 %all-reduce.4.cloned.1.call-done = f32[8,6144]{1,0:T(8,128)} async-done(((f32[8,6144]{1,0:T(8,128)}), f32[8,6144]{1,0:T(8,128)}) %all-reduce.4.cloned.1.call-update) | async-done | bytes 196624 | tf_op jit(solution)/shard_map/psum | solution.py:71
  224.5 8.4 %collective-permute-start.6 = (f32[8,768]{1,0:T(8,128)S(1)}, f32[8,768]{1,0:T(8,128)S(1)}, u32[]{:S(2)}, u32[]{:S(2)}) collective-permute-start(f32[8,768]{1,0:T(8,128)S(1)} %constant_dynamic-slice_fusion), channel_id=1, source_target_pairs={{0,8},{8,16},{16,24},{24,32},{32,40},{40,48},{48,56},{56,64},{64,7... | collective-permute-start | bytes 73736 | tf_op jit(solution)/shard_map/ppermute | solution.py:11
  234.5 2.4 collective-permute-start.7
  237.2 99.4 %psum.29 = bf16[32,128]{1,0:T(8,128)(2,1)S(1)} all-reduce(f32[32,128]{1,0:T(8,128)S(1)} %fusion.12), channel_id=1, replica_groups=mesh['blk'=64,'row'=8] {'blk','row'}, use_global_device_ids=true, to_apply=%region_5.6 | all-reduce | flops 4096 | bytes 24576 | tf_op jit(solution)/shard_map/psum | solution.py:44
  336.6 3.7 collective-permute-start.8
  340.4 3.8 collective-permute-done.8
  344.2 3.0 collective-permute-start.9
  347.6 2.4 collective-permute-done.9
  350.0 2.3 collective-permute-start.10
  352.3 2.8 fusion.23
  355.1 1.6 collective-permute-done.10
  356.7 5.8 %collective-permute-start.11 = (f32[8,768]{1,0:T(8,128)S(1)}, f32[8,768]{1,0:T(8,128)S(1)}, u32[]{:S(2)}, u32[]{:S(2)}) collective-permute-start(f32[8,768]{1,0:T(8,128)S(1)} %broadcast_select_fusion.10), channel_id=1, source_target_pairs={{0,256},{8,264},{16,272},{24,280},{32,288},{40,296},{48,304},{56,3... | collective-permute-start | bytes 73736 | tf_op jit(solution)/shard_map/ppermute | solution.py:11
  362.5 1.7 fusion.25
  364.1 1.0 collective-permute-done.11
  365.1 2.4 multiply_reduce_fusion.4
  367.5 99.9 %all-reduce.1 = (f32[8,128]{1,0:T(8,128)S(1)}, f32[8]{0:T(128)S(1)}) all-reduce(f32[8,128]{1,0:T(8,128)S(1)} %fusion.10, f32[8]{0:T(128)S(1)} %get-tuple-element.10), channel_id=1, replica_groups=mesh['blk'=64,'row'=8] {'blk','row'}, use_global_device_ids=true, to_apply=%region_7.8 | all-reduce | flops 1032 | bytes 8256 | tf_op jit(solution)/shard_map/psum | solution.py:49
  (44 shorter events, 10.0 us)
Async XLA Ops:
  7.2 216.6 %all-reduce.4.cloned.1.call-start = ((), (), s32[]{:S(2)}) async-start(), calls=%async_computation | async-start | bytes 393216 | tf_op jit(solution)/shard_map/psum | solution.py:71
  9.6 9.7 %collective-permute-start = (bf16[40,768]{1,0:T(8,128)(2,1)S(1)}, bf16[40,768]{1,0:T(8,128)(2,1)S(1)}, u32[]{:S(2)}, u32[]{:S(2)}) collective-permute-start(bf16[40,768]{1,0:T(8,128)(2,1)S(1)} %pad_maximum_fusion), channel_id=1, source_target_pairs={{0,504},{8,0},{16,8},{24,16},{32,24},{40,32},{48,40},{56,48},{64,5... | collective-permute-start | bytes 184328 | tf_op jit(solution)/shard_map/ppermute | solution.py:11
  20.0 12.4 %collective-permute-start.1 = (bf16[40,768]{1,0:T(8,128)(2,1)S(1)}, bf16[40,768]{1,0:T(8,128)(2,1)S(1)}, u32[]{:S(2)}, u32[]{:S(2)}) collective-permute-start(bf16[40,768]{1,0:T(8,128)(2,1)S(1)} %broadcast_select_fusion), channel_id=1, source_target_pairs={{0,496},{8,504},{16,0},{24,8},{32,16},{40,24},{48,32},{56,40},{64,... | collective-permute-start | bytes 184328 | tf_op jit(solution)/shard_map/ppermute | solution.py:11
  32.4 5.9 %collective-permute-start.2 = (bf16[40,768]{1,0:T(8,128)(2,1)S(1)}, bf16[40,768]{1,0:T(8,128)(2,1)S(1)}, u32[]{:S(2)}, u32[]{:S(2)}) collective-permute-start(bf16[40,768]{1,0:T(8,128)(2,1)S(1)} %broadcast_select_fusion.1), channel_id=1, source_target_pairs={{0,480},{8,488},{16,496},{24,504},{32,0},{40,8},{48,16},{56,24},{6... | collective-permute-start | bytes 184328 | tf_op jit(solution)/shard_map/ppermute | solution.py:11
  38.3 5.5 %collective-permute-start.3 = (bf16[40,768]{1,0:T(8,128)(2,1)S(1)}, bf16[40,768]{1,0:T(8,128)(2,1)S(1)}, u32[]{:S(2)}, u32[]{:S(2)}) collective-permute-start(bf16[40,768]{1,0:T(8,128)(2,1)S(1)} %broadcast_select_fusion.2), channel_id=1, source_target_pairs={{0,448},{8,456},{16,464},{24,472},{32,480},{40,488},{48,496},{56,5... | collective-permute-start | bytes 184328 | tf_op jit(solution)/shard_map/ppermute | solution.py:11
  43.8 6.9 %collective-permute-start.4 = (bf16[40,768]{1,0:T(8,128)(2,1)S(1)}, bf16[40,768]{1,0:T(8,128)(2,1)S(1)}, u32[]{:S(2)}, u32[]{:S(2)}) collective-permute-start(bf16[40,768]{1,0:T(8,128)(2,1)S(1)} %broadcast_select_fusion.3), channel_id=1, source_target_pairs={{0,384},{8,392},{16,400},{24,408},{32,416},{40,424},{48,432},{56,4... | collective-permute-start | bytes 184328 | tf_op jit(solution)/shard_map/ppermute | solution.py:11
  50.7 9.5 %collective-permute-start.5 = (bf16[40,768]{1,0:T(8,128)(2,1)S(1)}, bf16[40,768]{1,0:T(8,128)(2,1)S(1)}, u32[]{:S(2)}, u32[]{:S(2)}) collective-permute-start(bf16[40,768]{1,0:T(8,128)(2,1)S(1)} %broadcast_select_fusion.4), channel_id=1, source_target_pairs={{0,256},{8,264},{16,272},{24,280},{32,288},{40,296},{48,304},{56,3... | collective-permute-start | bytes 184328 | tf_op jit(solution)/shard_map/ppermute | solution.py:11
  100.4 3.8 copy-start.3
  100.6 1.6 copy-start.5
  104.3 3.8 copy-start.2
  105.9 1.7 copy-start
  108.0 128.8 %copy-start.6 = (s32[128]{0:T(128)S(1)}, s32[128]{0:T(128)}, u32[]{:S(2)}) copy-start(s32[128]{0:T(128)} %param.9) | copy-start | bytes 1540
  108.6 0.7 copy-start.4
  224.5 9.3 %collective-permute-start.6 = (f32[8,768]{1,0:T(8,128)S(1)}, f32[8,768]{1,0:T(8,128)S(1)}, u32[]{:S(2)}, u32[]{:S(2)}) collective-permute-start(f32[8,768]{1,0:T(8,128)S(1)} %constant_dynamic-slice_fusion), channel_id=1, source_target_pairs={{0,8},{8,16},{16,24},{24,32},{32,40},{40,48},{48,56},{56,64},{64,7... | collective-permute-start | bytes 73736 | tf_op jit(solution)/shard_map/ppermute | solution.py:11
  234.5 102.1 %collective-permute-start.7 = (f32[8,768]{1,0:T(8,128)S(1)}, f32[8,768]{1,0:T(8,128)S(1)}, u32[]{:S(2)}, u32[]{:S(2)}) collective-permute-start(f32[8,768]{1,0:T(8,128)S(1)} %broadcast_select_fusion.6), channel_id=1, source_target_pairs={{0,16},{8,24},{16,32},{24,40},{32,48},{40,56},{48,64},{56,72},{64,... | collective-permute-start | bytes 73736 | tf_op jit(solution)/shard_map/ppermute | solution.py:11
  336.6 7.6 %collective-permute-start.8 = (f32[8,768]{1,0:T(8,128)S(1)}, f32[8,768]{1,0:T(8,128)S(1)}, u32[]{:S(2)}, u32[]{:S(2)}) collective-permute-start(f32[8,768]{1,0:T(8,128)S(1)} %broadcast_select_fusion.7), channel_id=1, source_target_pairs={{0,32},{8,40},{16,48},{24,56},{32,64},{40,72},{48,80},{56,88},{64,... | collective-permute-start | bytes 73736 | tf_op jit(solution)/shard_map/ppermute | solution.py:11
  344.2 5.8 %collective-permute-start.9 = (f32[8,768]{1,0:T(8,128)S(1)}, f32[8,768]{1,0:T(8,128)S(1)}, u32[]{:S(2)}, u32[]{:S(2)}) collective-permute-start(f32[8,768]{1,0:T(8,128)S(1)} %broadcast_select_fusion.8), channel_id=1, source_target_pairs={{0,64},{8,72},{16,80},{24,88},{32,96},{40,104},{48,112},{56,120},{... | collective-permute-start | bytes 73736 | tf_op jit(solution)/shard_map/ppermute | solution.py:11
  347.6 14.9 %copy-start.1 = (bf16[768,2048]{1,0:T(8,128)(2,1)S(1)}, bf16[768,2048]{1,0:T(8,128)(2,1)}, u32[]{:S(2)}) copy-start(bf16[768,2048]{1,0:T(8,128)(2,1)} %copy-done) | copy-start | bytes 9437188
  350.0 6.7 %collective-permute-start.10 = (f32[8,768]{1,0:T(8,128)S(1)}, f32[8,768]{1,0:T(8,128)S(1)}, u32[]{:S(2)}, u32[]{:S(2)}) collective-permute-start(f32[8,768]{1,0:T(8,128)S(1)} %broadcast_select_fusion.9), channel_id=1, source_target_pairs={{0,128},{8,136},{16,144},{24,152},{32,160},{40,168},{48,176},{56,1... | collective-permute-start | bytes 73736 | tf_op jit(solution)/shard_map/ppermute | solution.py:11
  356.7 8.5 %collective-permute-start.11 = (f32[8,768]{1,0:T(8,128)S(1)}, f32[8,768]{1,0:T(8,128)S(1)}, u32[]{:S(2)}, u32[]{:S(2)}) collective-permute-start(f32[8,768]{1,0:T(8,128)S(1)} %broadcast_select_fusion.10), channel_id=1, source_target_pairs={{0,256},{8,264},{16,272},{24,280},{32,288},{40,296},{48,304},{56,3... | collective-permute-start | bytes 73736 | tf_op jit(solution)/shard_map/ppermute | solution.py:11
Sparse Core Ops, SparseCore 0:
  109.4 114.3 all-reduce.3
where the time goes:
time: 476 us; the launch traced here: 475 us
  blocking collectives  240 us (50%)
  waiting for transfers between devices  142 us (30%)
  starting transfers between devices  56.8 us (12%)
  between operations  14.9 us (3%)
  matrix products  13.8 us (3%)
    psum x1, waiting for transfers between devices, body(): summed = lax.psum(backward, 'row')  114 us
    psum x1, blocking collectives, body(): projection = lax.psum(projection_part, ('blk', 'row')) * projection_scale  99.9 us
    psum x1, blocking collectives, body(): pivot_feat = lax.psum(pivot_part, ('blk', 'row')).astype(jnp.bfloat16)  99.4 us
    ppermute x12, starting transfers between devices, passed_along(): return lax.ppermute(x, axis, [(i, (i + by) % peers) for i in range(peers)])  56.8 us
    all_gather x1, blocking collectives, body(): shard_piece = lax.all_gather(partner_data, 'row', axis=1, tiled=True)  40.2 us
    ppermute x12, waiting for transfers between devices, passed_along(): return lax.ppermute(x, axis, [(i, (i + by) % peers) for i in range(peers)])  27.6 us
  transfers between devices with their start and end apart: 13, of which 12 were waited for; matrix products, arithmetic and copies ran while one was open for 1% of the time, Pallas kernels for 0%

commit v1 on v0

v1 whole, which is shorter than its diff:
```python
import math

import jax
import jax.numpy as jnp
from jax import lax
from jax.sharding import Mesh
from jax.sharding import PartitionSpec as P

Y, ZLO, CORE, ZHI, X = 8, 4, 2, 2, 4
GROUP_AXES = ("y", "zlo", "core")
ALL_AXES = ("y", "zlo", "core", "zhi", "x")
MAX_SHIFT = 31


def shifted(x, axes, by):
    peers = lax.axis_size(axes)
    return lax.ppermute(x, axes, [(i, (i + by) % peers) for i in range(peers)])


def gathered(x, axes):
    peers = lax.axis_size(axes)
    return lax.all_to_all(jnp.broadcast_to(x[None], (peers,) + x.shape), axes, 0, 0)


def square_norm(scaled_feat):
    wide = scaled_feat.astype(jnp.float32)
    return jnp.sum(wide * wide, axis=0)


def kernel_block(row_feat, row_norm, col_feat, col_norm):
    inner_prod = jnp.dot(row_feat.T, col_feat, preferred_element_type=jnp.float32)
    distance = row_norm[:, None] + col_norm[None, :] - 2.0 * inner_prod
    return jnp.exp(-0.5 * distance).astype(jnp.bfloat16)


def body(features, probes, inverse_scales, round_index, pivots):
    feat_count, row_count = features.shape
    group_count = lax.axis_size(GROUP_AXES)
    row_devices = lax.axis_size(("zhi", "x"))
    block_points = row_count * row_devices
    total_points = block_points * group_count

    scaled = (features * jnp.sqrt(inverse_scales)[:, None]).astype(jnp.bfloat16)
    packed = jnp.concatenate([scaled, probes], axis=0)

    first_point = lax.axis_index(ALL_AXES) * row_count
    points = first_point + jnp.arange(row_count, dtype=jnp.int32)
    pivot_mask = (points[:, None] == pivots[None, :]).astype(jnp.bfloat16)
    pivot_part = jnp.dot(scaled, pivot_mask, preferred_element_type=jnp.float32).astype(jnp.bfloat16)
    pivot_some = jnp.sum(gathered(pivot_part, ("y", "x")), axis=0)

    def both_ways(shift):
        def branch(data):
            return shifted(data, GROUP_AXES, -shift), shifted(data, GROUP_AXES, shift)

        return branch

    after, before = lax.switch(
        round_index[0] - 1, [both_ways(k) for k in range(1, MAX_SHIFT + 1)], packed
    )
    paired = shifted(packed, ("zhi",), 1)
    pivot_feat = jnp.sum(gathered(pivot_some, ("zlo", "core", "zhi")), axis=0)
    cols = gathered(jnp.stack([after, before]), ("x",)).reshape(-1, packed.shape[0], row_count)

    own_norm = square_norm(scaled)
    pivot_kernel = kernel_block(scaled, own_norm, pivot_feat, square_norm(pivot_feat))
    projection_part = jnp.dot(probes, pivot_kernel, preferred_element_type=jnp.float32)

    rows = jnp.concatenate([packed, paired], axis=1)
    row_feat = rows[:feat_count]
    row_probe = rows[feat_count:]
    row_norm = square_norm(row_feat)
    total = jnp.zeros((probes.shape[0], rows.shape[1]), jnp.float32)
    for piece in range(cols.shape[0]):
        col_feat = cols[piece, :feat_count]
        col_probe = cols[piece, feat_count:]
        kernel = kernel_block(col_feat, square_norm(col_feat), row_feat, row_norm)
        total = total + jnp.dot(col_probe, kernel, preferred_element_type=jnp.float32)

    total = 8.0 / math.sqrt(block_points) * total
    product = total[:, :row_count] + shifted(total[:, row_count:], ("zhi",), 1)
    quadratic_part = jnp.sum(row_probe.astype(jnp.float32) * total, axis=1)
    sums = jnp.concatenate(
        [projection_part, jnp.broadcast_to(quadratic_part[:, None], projection_part.shape)], axis=1
    )
    sums = jnp.sum(gathered(sums, ("y", "x")), axis=0)
    sums = jnp.sum(gathered(sums, ("zlo", "core", "zhi")), axis=0)
    rank = projection_part.shape[1]
    projection = sums[:, :rank] * (8.0 / math.sqrt(total_points))
    quadratic = sums[:, rank] / math.sqrt(total_points)
    return product, projection, quadratic


def solution(mesh):
    fine = Mesh(mesh.devices.reshape(Y, ZLO, CORE, ZHI, X), ALL_AXES)
    split = P(None, ALL_AXES)
    return jax.shard_map(
        body,
        mesh=fine,
        in_specs=(split, split, P(), P(), P()),
        out_specs=(split, P(), P()),
        check_vma=False,
    )
```

time: 476 us -> 134 us (0.28)
  blocking collectives: 240 us -> 0 us
  waiting for transfers between devices: 142 us -> 35 us
  starting transfers between devices: 56.8 us -> 74.2 us
  between operations: 14.9 us -> 1.39 us
    psum x2 -> x0, blocking collectives: 199 us -> none  [the longest x1 99.9 us: body(): projection = lax.psum(projection_part, ('blk', 'row')) * projection_scale]
    psum x1 -> x0, waiting for transfers between devices: 114 us -> none  [body(): summed = lax.psum(backward, 'row')]
    all_gather x1 -> x0, blocking collectives: 40.2 us -> none  [body(): shard_piece = lax.all_gather(partner_data, 'row', axis=1, tiled=True)]
    all_to_all x0 -> x5, starting transfers between devices: none -> 39.9 us  [gathered(): lax.all_to_all(jnp.broadcast_to(x[None], (peers,) + x.shape), axes, 0, 0)]
    all_to_all x0 -> x5, waiting for transfers between devices: none -> 30.6 us  [gathered(): lax.all_to_all(jnp.broadcast_to(x[None], (peers,) + x.shape), axes, 0, 0)]
    ppermute x12 -> x4, waiting for transfers between devices: 27.6 us -> 4.43 us  [shifted(): return lax.ppermute(x, axes, [(i, (i + by) % peers) for i in range(peers)])]
    ppermute x12 -> x4, starting transfers between devices: 56.8 us -> 34.3 us  [shifted(): return lax.ppermute(x, axes, [(i, (i + by) % peers) for i in range(peers)])]
    dot_general x10 -> x9, matrix products: 13.4 us -> 12 us  [the longest x8 11.7 us: body(): jnp.dot(col_probe, kernel, preferred_element_type=jnp.float32)]
  transfers between devices with their start and end apart: 13 -> 9, of which waited for: 12 -> 6; matrix products, arithmetic and copies ran while one was open for 1% -> 11% of each run, Pallas kernels for 0% -> 0%
where the time goes in v1:
time: 134 us; the launch traced here: 133 us
  starting transfers between devices  74.2 us (55%)
  waiting for transfers between devices  35 us (26%)
  matrix products  12.4 us (9%)
  other arithmetic  5.37 us (4%)
  local copies, waits for them, and re-layouts  4.37 us (3%)
  between operations  1.39 us (1%)
    all_to_all x5, starting transfers between devices, gathered(): lax.all_to_all(jnp.broadcast_to(x[None], (peers,) + x.shape), axes, 0, 0)  39.9 us
    ppermute x4, starting transfers between devices, shifted(): return lax.ppermute(x, axes, [(i, (i + by) % peers) for i in range(peers)])  34.3 us
    all_to_all x5, waiting for transfers between devices, gathered(): lax.all_to_all(jnp.broadcast_to(x[None], (peers,) + x.shape), axes, 0, 0)  30.6 us
    dot_general x8, matrix products, body(): jnp.dot(col_probe, kernel, preferred_element_type=jnp.float32)  11.7 us
    ppermute x4, waiting for transfers between devices, shifted(): return lax.ppermute(x, axes, [(i, (i + by) % peers) for i in range(peers)])  4.43 us
    broadcast_in_dim x5, local copies, waits for them, and re-layouts, gathered(): jnp.broadcast_to(x[None], (peers,) + x.shape)  3.63 us
  transfers between devices with their start and end apart: 9, of which 6 were waited for; matrix products, arithmetic and copies ran while one was open for 11% of the time, Pallas kernels for 0%

profile of v1, /device:TPU:1, one launch (start us, length us, event | category | flops | bytes accessed | tf_op | source)
XLA Modules:
  0.0 132.8 jit_solution(2488461971504353778)
XLA Ops:
  0.6 0.7 sqrt.3
  1.3 1.0 multiply_reduce_fusion.1
  2.3 1.3 %pad_maximum_fusion.2 = bf16[40,768]{1,0:T(8,128)(2,1)} fusion(bf16[8,768]{1,0:T(8,128)(2,1)} %param.37, bf16[32,768]{1,0:T(8,128)(2,1)S(1)} %get-tuple-element.49), kind=kLoop, calls=%fused_computation.46 | loop fusion | flops 122880 | bytes 122880 | tf_op jit(solution)/shard_map/concatenate | solution.py:44
  3.6 11.5 %collective-permute-start.62 = (bf16[40,768]{1,0:T(8,128)(2,1)}, bf16[40,768]{1,0:T(8,128)(2,1)S(1)}, u32[]{:S(2)}, u32[]{:S(2)}) collective-permute-start(bf16[40,768]{1,0:T(8,128)(2,1)} %pad_maximum_fusion.2), channel_id=1, source_target_pairs={{0,4},{4,0},{1,5},{5,1},{2,6},{6,2},{3,7},{7,3},{8,12},{12,8},{9,1... | collective-permute-start | bytes 184328 | tf_op jit(solution)/shard_map/ppermute | solution.py:17
  15.7 24.8 %conditional.1 = (bf16[1,40,768]{2,1,0:T(8,128)(2,1)}, bf16[1,40,768]{2,1,0:T(8,128)(2,1)}) conditional(s32[]{:T(128)} %bitcast.62, bf16[40,768]{1,0:T(8,128)(2,1)} %pad_maximum_fusion.2, bf16[40,768]{1,0:T(8,128)(2,1)} %pad_maximum_fusion.2, bf16[40,768]{1,0:T(8,128)(2,1)} %pad_maximum_fusion.2, ...), branch_computations={%region_0.0_spmd, %region_1.0_spmd, %region_2.0_spmd, %region_3.0_... | conditional | bytes 491616 | solution.py:58
  15.8 13.3 %collective-permute-start.38 = (bf16[40,768]{1,0:T(8,128)(2,1)}, bf16[40,768]{1,0:T(8,128)(2,1)}, u32[]{:S(2)}, u32[]{:S(2)}) collective-permute-start(bf16[40,768]{1,0:T(8,128)(2,1)} %param.19), channel_id=1, source_target_pairs={{0,352},{8,360},{16,368},{24,376},{32,384},{40,392},{48,400},{56,4... | collective-permute-start | bytes 184328 | tf_op jit(solution)/shard_map/cond/branch_19_fun/ppermute | solution.py:17
  29.0 7.1 %collective-permute-start.39 = (bf16[40,768]{1,0:T(8,128)(2,1)}, bf16[40,768]{1,0:T(8,128)(2,1)}, u32[]{:S(2)}, u32[]{:S(2)}) collective-permute-start(bf16[40,768]{1,0:T(8,128)(2,1)} %param.19), channel_id=1, source_target_pairs={{0,160},{8,168},{16,176},{24,184},{32,192},{40,200},{48,208},{56,2... | collective-permute-start | bytes 184328 | tf_op jit(solution)/shard_map/cond/branch_19_fun/ppermute | solution.py:17
  36.5 4.0 %collective-permute-done.39 = bf16[40,768]{1,0:T(8,128)(2,1)} collective-permute-done((bf16[40,768]{1,0:T(8,128)(2,1)}, bf16[40,768]{1,0:T(8,128)(2,1)}, u32[]{:S(2)}, u32[]{:S(2)}) %collective-permute-start.39) | collective-permute-done | bytes 61472 | tf_op jit(solution)/shard_map/cond/branch_19_fun/ppermute | solution.py:17
  40.5 0.9 pad_maximum_fusion
  41.4 0.8 broadcast_in_dim.12
  42.2 4.4 %all-to-all-start = ((bf16[4,2,40,768]{3,2,1,0:T(8,128)(2,1)}), bf16[4,2,40,768]{3,2,1,0:T(8,128)(2,1)S(1)}, u32[]{:S(2)}, u32[]{:S(2)}) async-start(bf16[4,2,40,768]{3,2,1,0:T(8,128)(2,1)} %broadcast_in_dim.12), calls=%async_computation | async-start | bytes 983040 | tf_op jit(solution)/shard_map/all_to_all | solution.py:22
  47.0 6.4 %all-to-all-done = bf16[4,2,40,768]{3,2,1,0:T(8,128)(2,1)S(1)} async-done(((bf16[4,2,40,768]{3,2,1,0:T(8,128)(2,1)}), bf16[4,2,40,768]{3,2,1,0:T(8,128)(2,1)S(1)}, u32[]{:S(2)}, u32[]{:S(2)}) %all-to-all-start) | async-done | bytes 491552 | tf_op jit(solution)/shard_map/all_to_all | solution.py:22
  53.4 0.7 broadcast_in_dim.13
  54.1 9.5 %all-to-all-start.1 = ((bf16[32,32,128]{2,1,0:T(8,128)(2,1)}), bf16[32,32,128]{2,1,0:T(8,128)(2,1)S(1)}, u32[]{:S(2)}, u32[]{:S(2)}) async-start(bf16[32,32,128]{2,1,0:T(8,128)(2,1)} %broadcast_in_dim.13), calls=%async_computation.1 | async-start | bytes 524288 | tf_op jit(solution)/shard_map/all_to_all | solution.py:22
  63.8 1.4 %fusion.1 = f32[8,1536]{1,0:T(8,128)S(1)} fusion(f32[1536]{0:T(1024)S(1)} %multiply_reduce_fusion, f32[768]{0:T(1024)S(1)} %get-tuple-element.47, bf16[8,40,768]{2,1,0:T(8,128)(2,1)S(1)} %bitcast.147, bf16[40,1536]{1,0:T(8,128)(2,1)S(1)} %pad_maximum_fusion.1), kind=kOutput, calls=%fused_computation.16 | convolution fusion | flops 100270080 | bytes 221184 | tf_op jit(solution)/shard_map/dot_general | solution.py:78
  65.2 1.4 %convolution_add_fusion.6 = f32[8,1536]{1,0:T(8,128)S(1)} fusion(f32[8,1536]{1,0:T(8,128)S(1)} %fusion.1, f32[768]{0:T(1024)S(1)} %get-tuple-element.46, f32[1536]{0:T(1024)S(1)} %multiply_reduce_fusion, bf16[8,40,768]{2,1,0:T(8,128)(2,1)S(1)} %bitcast.148, bf16[40,1536]{1,0:T(8,128)(2,1)S(1)} %pad_maximum_fusion.1), kind=kOutput, calls=%fused_computation.15 | convolution fusion | flops 100282368 | bytes 270336 | tf_op jit(solution)/shard_map/dot_general | solution.py:78
  66.6 1.4 %convolution_add_fusion.5 = f32[8,1536]{1,0:T(8,128)S(1)} fusion(f32[8,1536]{1,0:T(8,128)S(1)} %convolution_add_fusion.6, f32[768]{0:T(1024)S(1)} %get-tuple-element.45, f32[1536]{0:T(1024)S(1)} %multiply_reduce_fusion, bf16[8,40,768]{2,1,0:T(8,128)(2,1)S(1)} %bitcast.149, bf16[40,1536]{1,0:T(8,128)(2,1)S(1)} %pad_maximum_fusion.1), kind=kOutput, calls=%fused_computation.14 | convolution fusion | flops 100282368 | bytes 270336 | tf_op jit(solution)/shard_map/dot_general | solution.py:78
  68.1 1.4 %convolution_add_fusion.4 = f32[8,1536]{1,0:T(8,128)S(1)} fusion(f32[8,1536]{1,0:T(8,128)S(1)} %convolution_add_fusion.5, f32[768]{0:T(1024)S(1)} %get-tuple-element.44, f32[1536]{0:T(1024)S(1)} %multiply_reduce_fusion, bf16[8,40,768]{2,1,0:T(8,128)(2,1)S(1)} %bitcast.150, bf16[40,1536]{1,0:T(8,128)(2,1)S(1)} %pad_maximum_fusion.1), kind=kOutput, calls=%fused_computation.13 | convolution fusion | flops 100282368 | bytes 270336 | tf_op jit(solution)/shard_map/dot_general | solution.py:78
  69.5 1.4 %convolution_add_fusion.3 = f32[8,1536]{1,0:T(8,128)S(1)} fusion(f32[8,1536]{1,0:T(8,128)S(1)} %convolution_add_fusion.4, f32[768]{0:T(1024)S(1)} %get-tuple-element.43, f32[1536]{0:T(1024)S(1)} %multiply_reduce_fusion, bf16[8,40,768]{2,1,0:T(8,128)(2,1)S(1)} %bitcast.151, bf16[40,1536]{1,0:T(8,128)(2,1)S(1)} %pad_maximum_fusion.1), kind=kOutput, calls=%fused_computation.12 | convolution fusion | flops 100282368 | bytes 270336 | tf_op jit(solution)/shard_map/dot_general | solution.py:78
  71.0 1.4 %convolution_add_fusion.2 = f32[8,1536]{1,0:T(8,128)S(1)} fusion(f32[8,1536]{1,0:T(8,128)S(1)} %convolution_add_fusion.3, f32[768]{0:T(1024)S(1)} %get-tuple-element.42, f32[1536]{0:T(1024)S(1)} %multiply_reduce_fusion, bf16[8,40,768]{2,1,0:T(8,128)(2,1)S(1)} %bitcast.152, bf16[40,1536]{1,0:T(8,128)(2,1)S(1)} %pad_maximum_fusion.1), kind=kOutput, calls=%fused_computation.11 | convolution fusion | flops 100282368 | bytes 270336 | tf_op jit(solution)/shard_map/dot_general | solution.py:78
  72.4 1.4 %convolution_add_fusion.1 = f32[8,1536]{1,0:T(8,128)S(1)} fusion(f32[8,1536]{1,0:T(8,128)S(1)} %convolution_add_fusion.2, f32[768]{0:T(1024)S(1)} %get-tuple-element.41, f32[1536]{0:T(1024)S(1)} %multiply_reduce_fusion, bf16[8,40,768]{2,1,0:T(8,128)(2,1)S(1)} %bitcast.153, bf16[40,1536]{1,0:T(8,128)(2,1)S(1)} %pad_maximum_fusion.1), kind=kOutput, calls=%fused_computation.10 | convolution fusion | flops 100282368 | bytes 270336 | tf_op jit(solution)/shard_map/dot_general | solution.py:78
  73.9 0.7 broadcast_in_dim.14
  74.6 12.2 %all-to-all-start.2 = ((bf16[16,32,128]{2,1,0:T(8,128)(2,1)}), bf16[16,32,128]{2,1,0:T(8,128)(2,1)S(1)}, u32[]{:S(2)}, u32[]{:S(2)}) async-start(bf16[16,32,128]{2,1,0:T(8,128)(2,1)} %broadcast_in_dim.14), calls=%async_computation.2 | async-start | bytes 262144 | tf_op jit(solution)/shard_map/all_to_all | solution.py:22
  86.8 1.6 %multiply_reduce_fusion.10 = (f32[8]{0:T(128)S(1)}, f32[8,1536]{1,0:T(8,128)S(1)}) fusion(bf16[40,768]{1,0:T(8,128)(2,1)S(1)} %collective-permute-done.62, bf16[8,768]{1,0:T(8,128)(2,1)S(1)} %copy-done, bf16[32,768]{1,0:T(8,128)(2,1)S(1)} %get-tuple-element.49, f32[8,1536]{1,0:T(8,128)S(1)} %convolution_add_fusion.1, f32[768]{0:T(1024)S(1)} %get-tuple-element.40, ...), kind=kOutput, calls=%fused_computation.55 | convolution fusion | flops 100392952 | bytes 393248 | tf_op jit(solution)/shard_map/dot_general | solution.py:78
  88.3 7.4 %all-to-all-done.2 = bf16[16,32,128]{2,1,0:T(8,128)(2,1)S(1)} async-done(((bf16[16,32,128]{2,1,0:T(8,128)(2,1)}), bf16[16,32,128]{2,1,0:T(8,128)(2,1)S(1)}, u32[]{:S(2)}, u32[]{:S(2)}) %all-to-all-start.2) | async-done | bytes 131104 | tf_op jit(solution)/shard_map/all_to_all | solution.py:22
  96.2 0.7 broadcast_in_dim.16
  97.0 8.1 %all-to-all-start.3 = ((f32[32,8,256]{2,1,0:T(8,128)}), f32[32,8,256]{2,1,0:T(8,128)S(1)}, u32[]{:S(2)}, u32[]{:S(2)}) async-start(f32[32,8,256]{2,1,0:T(8,128)} %broadcast_in_dim.16), calls=%async_computation.3 | async-start | bytes 524288 | tf_op jit(solution)/shard_map/all_to_all | solution.py:22
  105.1 2.5 %collective-permute-start.63 = (f32[8,768]{1,0:T(8,128)S(1)}, f32[8,768]{1,0:T(8,128)S(1)}, u32[]{:S(2)}, u32[]{:S(2)}) collective-permute-start(f32[8,768]{1,0:T(8,128)S(1)} %slice.106), channel_id=1, source_target_pairs={{0,4},{4,0},{1,5},{5,1},{2,6},{6,2},{3,7},{7,3},{8,12},{12,8},{9,1... | collective-permute-start | bytes 73736 | tf_op jit(solution)/shard_map/ppermute | solution.py:17
  107.6 8.7 %all-to-all-done.3 = f32[32,8,256]{2,1,0:T(8,128)S(1)} async-done(((f32[32,8,256]{2,1,0:T(8,128)}), f32[32,8,256]{2,1,0:T(8,128)S(1)}, u32[]{:S(2)}, u32[]{:S(2)}) %all-to-all-start.3) | async-done | bytes 262176 | tf_op jit(solution)/shard_map/all_to_all | solution.py:22
  116.3 0.7 broadcast_in_dim.17
  117.0 5.7 %all-to-all-start.4 = ((f32[16,8,256]{2,1,0:T(8,128)}), f32[16,8,256]{2,1,0:T(8,128)S(1)}, u32[]{:S(2)}, u32[]{:S(2)}) async-start(f32[16,8,256]{2,1,0:T(8,128)} %broadcast_in_dim.17), calls=%async_computation.4 | async-start | bytes 262144 | tf_op jit(solution)/shard_map/all_to_all | solution.py:22
  123.4 8.2 %all-to-all-done.4 = f32[16,8,256]{2,1,0:T(8,128)S(1)} async-done(((f32[16,8,256]{2,1,0:T(8,128)}), f32[16,8,256]{2,1,0:T(8,128)S(1)}, u32[]{:S(2)}, u32[]{:S(2)}) %all-to-all-start.4) | async-done | bytes 131104 | tf_op jit(solution)/shard_map/all_to_all | solution.py:22
  (25 shorter events, 3.4 us)
Async XLA Ops:
  3.6 43.3 %collective-permute-start.62 = (bf16[40,768]{1,0:T(8,128)(2,1)}, bf16[40,768]{1,0:T(8,128)(2,1)S(1)}, u32[]{:S(2)}, u32[]{:S(2)}) collective-permute-start(bf16[40,768]{1,0:T(8,128)(2,1)} %pad_maximum_fusion.2), channel_id=1, source_target_pairs={{0,4},{4,0},{1,5},{5,1},{2,6},{6,2},{3,7},{7,3},{8,12},{12,8},{9,1... | collective-permute-start | bytes 184328 | tf_op jit(solution)/shard_map/ppermute | solution.py:17
  15.8 20.8 %collective-permute-start.38 = (bf16[40,768]{1,0:T(8,128)(2,1)}, bf16[40,768]{1,0:T(8,128)(2,1)}, u32[]{:S(2)}, u32[]{:S(2)}) collective-permute-start(bf16[40,768]{1,0:T(8,128)(2,1)} %param.19), channel_id=1, source_target_pairs={{0,352},{8,360},{16,368},{24,376},{32,384},{40,392},{48,400},{56,4... | collective-permute-start | bytes 184328 | tf_op jit(solution)/shard_map/cond/branch_19_fun/ppermute | solution.py:17
  29.0 11.5 %collective-permute-start.39 = (bf16[40,768]{1,0:T(8,128)(2,1)}, bf16[40,768]{1,0:T(8,128)(2,1)}, u32[]{:S(2)}, u32[]{:S(2)}) collective-permute-start(bf16[40,768]{1,0:T(8,128)(2,1)} %param.19), channel_id=1, source_target_pairs={{0,160},{8,168},{16,176},{24,184},{32,192},{40,200},{48,208},{56,2... | collective-permute-start | bytes 184328 | tf_op jit(solution)/shard_map/cond/branch_19_fun/ppermute | solution.py:17
  42.2 4.4 %copy-start.1 = (s32[128]{0:T(128)S(1)}, s32[128]{0:T(128)}, u32[]{:S(2)}) copy-start(s32[128]{0:T(128)} %param.40) | copy-start | bytes 1540
  42.2 4.7 %copy-start = (bf16[8,768]{1,0:T(8,128)(2,1)S(1)}, bf16[8,768]{1,0:T(8,128)(2,1)}, u32[]{:S(2)}) copy-start(bf16[8,768]{1,0:T(8,128)(2,1)} %param.37) | copy-start | bytes 36868
  42.2 11.2 %all-to-all-start = ((bf16[4,2,40,768]{3,2,1,0:T(8,128)(2,1)}), bf16[4,2,40,768]{3,2,1,0:T(8,128)(2,1)S(1)}, u32[]{:S(2)}, u32[]{:S(2)}) async-start(bf16[4,2,40,768]{3,2,1,0:T(8,128)(2,1)} %broadcast_in_dim.12), calls=%async_computation | async-start | bytes 983040 | tf_op jit(solution)/shard_map/all_to_all | solution.py:22
  54.1 19.7 %all-to-all-start.1 = ((bf16[32,32,128]{2,1,0:T(8,128)(2,1)}), bf16[32,32,128]{2,1,0:T(8,128)(2,1)S(1)}, u32[]{:S(2)}, u32[]{:S(2)}) async-start(bf16[32,32,128]{2,1,0:T(8,128)(2,1)} %broadcast_in_dim.13), calls=%async_computation.1 | async-start | bytes 524288 | tf_op jit(solution)/shard_map/all_to_all | solution.py:22
  74.6 21.1 %all-to-all-start.2 = ((bf16[16,32,128]{2,1,0:T(8,128)(2,1)}), bf16[16,32,128]{2,1,0:T(8,128)(2,1)S(1)}, u32[]{:S(2)}, u32[]{:S(2)}) async-start(bf16[16,32,128]{2,1,0:T(8,128)(2,1)} %broadcast_in_dim.14), calls=%async_computation.2 | async-start | bytes 262144 | tf_op jit(solution)/shard_map/all_to_all | solution.py:22
  97.0 19.3 %all-to-all-start.3 = ((f32[32,8,256]{2,1,0:T(8,128)}), f32[32,8,256]{2,1,0:T(8,128)S(1)}, u32[]{:S(2)}, u32[]{:S(2)}) async-start(f32[32,8,256]{2,1,0:T(8,128)} %broadcast_in_dim.16), calls=%async_computation.3 | async-start | bytes 524288 | tf_op jit(solution)/shard_map/all_to_all | solution.py:22
  105.1 17.6 %collective-permute-start.63 = (f32[8,768]{1,0:T(8,128)S(1)}, f32[8,768]{1,0:T(8,128)S(1)}, u32[]{:S(2)}, u32[]{:S(2)}) collective-permute-start(f32[8,768]{1,0:T(8,128)S(1)} %slice.106), channel_id=1, source_target_pairs={{0,4},{4,0},{1,5},{5,1},{2,6},{6,2},{3,7},{7,3},{8,12},{12,8},{9,1... | collective-permute-start | bytes 73736 | tf_op jit(solution)/shard_map/ppermute | solution.py:17
  117.0 14.5 %all-to-all-start.4 = ((f32[16,8,256]{2,1,0:T(8,128)}), f32[16,8,256]{2,1,0:T(8,128)S(1)}, u32[]{:S(2)}, u32[]{:S(2)}) async-start(f32[16,8,256]{2,1,0:T(8,128)} %broadcast_in_dim.17), calls=%async_computation.4 | async-start | bytes 262144 | tf_op jit(solution)/shard_map/all_to_all | solution.py:22

commit v2 on v1

v2 whole, which is shorter than its diff:
```python
import math

import jax
import jax.numpy as jnp
from jax import lax
from jax.sharding import Mesh
from jax.sharding import PartitionSpec as P

Y, ZLO, CORE, ZHI, X = 8, 4, 2, 2, 4
GROUP_AXES = ("y", "zlo", "core")
ALL_AXES = ("y", "zlo", "core", "zhi", "x")
SUM_AXES = (("y", "core"), ("zlo", "zhi", "x"))
MAX_SHIFT = 31


def crossed(x, axis, bit):
    return lax.ppermute(x, axis, [(i, i ^ bit) for i in range(lax.axis_size(axis))])


def gathered(x, axes):
    peers = lax.axis_size(axes)
    return lax.all_to_all(jnp.broadcast_to(x[None], (peers,) + x.shape), axes, 0, 0)


def from_partner(x, shift):
    groups, halves, width = lax.axis_size(GROUP_AXES), lax.axis_size("zhi"), lax.axis_size("x")
    pairs = []
    for group in range(groups):
        for half in range(halves):
            for place in range(width):
                way = 1 - 2 * ((place + group) % 2)
                source = (group + way * shift) % groups
                source = (source * halves + (half ^ place // 2)) * width + place
                pairs.append((source, (group * halves + half) * width + place))
    return lax.ppermute(x, ALL_AXES, pairs)


def square_norm(scaled_feat):
    wide = scaled_feat.astype(jnp.float32)
    return jnp.sum(wide * wide, axis=0)


def kernel_block(row_feat, row_norm, col_feat, col_norm):
    inner_prod = jnp.dot(row_feat.T, col_feat, preferred_element_type=jnp.float32)
    distance = row_norm[:, None] + col_norm[None, :] - 2.0 * inner_prod
    return jnp.exp(-0.5 * distance).astype(jnp.bfloat16)


def body(features, probes, inverse_scales, round_index, pivots):
    feat_count, row_count = features.shape
    probe_count = probes.shape[0]
    rank = pivots.shape[0]
    width = lax.axis_size("x")
    group_count = lax.axis_size(GROUP_AXES)
    block_points = row_count * lax.axis_size(("zhi", "x"))
    total_points = block_points * group_count
    product_scale = 8.0 / math.sqrt(block_points)

    scaled = (features * jnp.sqrt(inverse_scales)[:, None]).astype(jnp.bfloat16)
    packed = jnp.concatenate([scaled, probes], axis=0)
    quad = gathered(packed, "x")

    first_point = lax.axis_index(ALL_AXES) * row_count
    points = first_point + jnp.arange(row_count, dtype=jnp.int32)
    pivot_mask = (points[:, None] == pivots[None, :]).astype(jnp.bfloat16)
    pivot_part = jnp.dot(scaled, pivot_mask, preferred_element_type=jnp.float32).astype(jnp.bfloat16)

    def fetch(shift):
        def branch(data, part):
            some = jnp.sum(gathered(part, SUM_AXES[0]), axis=0)
            return from_partner(data, shift), some

        return branch

    pieces, pivot_some = lax.switch(
        round_index[0] - 1, [fetch(k) for k in range(1, MAX_SHIFT + 1)], quad, pivot_part
    )
    pivot_feat = jnp.sum(gathered(pivot_some, SUM_AXES[1]), axis=0)
    own_norm = square_norm(scaled)
    pivot_kernel = kernel_block(scaled, own_norm, pivot_feat, square_norm(pivot_feat))
    projection_part = jnp.dot(probes, pivot_kernel, preferred_element_type=jnp.float32)

    rows = quad.transpose(1, 0, 2).reshape(-1, width * row_count)
    row_feat = rows[:feat_count]
    row_probe = rows[feat_count:]
    row_norm = square_norm(row_feat)
    total = jnp.zeros((probe_count, width * row_count), jnp.float32)
    for place in range(width):
        col_feat = pieces[place, :feat_count]
        col_probe = pieces[place, feat_count:]
        kernel = kernel_block(col_feat, square_norm(col_feat), row_feat, row_norm)
        total = total + jnp.dot(col_probe, kernel, preferred_element_type=jnp.float32)
    total = product_scale * total
    quadratic_part = jnp.sum(row_probe.astype(jnp.float32) * total, axis=1)

    place = lax.axis_index("x")
    halves = total.reshape(probe_count, 2, 2 * row_count)
    kept = lax.dynamic_index_in_dim(halves, place // 2, 1, keepdims=False)
    given = lax.dynamic_index_in_dim(halves, 1 - place // 2, 1, keepdims=False)
    kept = kept + crossed(given, "x", 2)
    parts = kept.reshape(probe_count, 2, row_count)
    kept = lax.dynamic_index_in_dim(parts, place % 2, 1, keepdims=False)
    given = lax.dynamic_index_in_dim(parts, 1 - place % 2, 1, keepdims=False)
    product = kept + crossed(given, "x", 1)

    sums = jnp.concatenate(
        [projection_part, jnp.broadcast_to(quadratic_part[:, None], projection_part.shape)], axis=1
    )
    sums = jnp.sum(gathered(sums, SUM_AXES[0]), axis=0)
    sums = jnp.sum(gathered(sums, SUM_AXES[1]), axis=0)
    projection = sums[:, :rank] * (8.0 / math.sqrt(total_points))
    quadratic = sums[:, rank] / math.sqrt(total_points)
    return product, projection, quadratic


def solution(mesh):
    fine = Mesh(mesh.devices.reshape(Y, ZLO, CORE, ZHI, X), ALL_AXES)
    split = P(None, ALL_AXES)
    return jax.shard_map(
        body,
        mesh=fine,
        in_specs=(split, split, P(), P(), P()),
        out_specs=(split, P(), P()),
        check_vma=False,
    )
```

time: 134 us -> 107 us (0.80)
  starting transfers between devices: 74.2 us -> 52.1 us
  waiting for transfers between devices: 35 us -> 26.9 us
  matrix products: 12.4 us -> 14.7 us
    ppermute x4 -> x3, starting transfers between devices: 34.3 us -> 13.1 us  [the longest x2 8.1 us: crossed(): lax.ppermute(x, axis, [(i, i ^ bit) for i in range(lax.axis_size(axis))])]
    all_to_all x5, waiting for transfers between devices: 30.6 us -> 25.2 us  [gathered(): lax.all_to_all(jnp.broadcast_to(x[None], (peers,) + x.shape), axes, 0, 0)]
    ppermute x4 -> x3, waiting for transfers between devices: 4.43 us -> 1.73 us  [the longest x2 1.73 us: crossed(): lax.ppermute(x, axis, [(i, i ^ bit) for i in range(lax.axis_size(axis))])]
    dot_general x8 -> x4, matrix products: 11.7 us -> 14 us  [body(): jnp.dot(col_probe, kernel, preferred_element_type=jnp.float32)]
  transfers between devices with their start and end apart: 9 -> 8, of which waited for: 6 -> 5; matrix products, arithmetic and copies ran while one was open for 11% -> 15% of each run, Pallas kernels for 0% -> 0%
where the time goes in v2:
time: 107 us; the launch traced here: 106 us
  starting transfers between devices  52.1 us (49%)
  waiting for transfers between devices  26.9 us (25%)
  matrix products  14.7 us (14%)
  other arithmetic  5.62 us (5%)
  local copies, waits for them, and re-layouts  4.92 us (5%)
  between operations  1.47 us (1%)
    all_to_all x5, starting transfers between devices, gathered(): lax.all_to_all(jnp.broadcast_to(x[None], (peers,) + x.shape), axes, 0, 0)  38.9 us
    all_to_all x5, waiting for transfers between devices, gathered(): lax.all_to_all(jnp.broadcast_to(x[None], (peers,) + x.shape), axes, 0, 0)  25.2 us
    dot_general x4, matrix products, body(): jnp.dot(col_probe, kernel, preferred_element_type=jnp.float32)  14 us
    ppermute x2, starting transfers between devices, crossed(): lax.ppermute(x, axis, [(i, i ^ bit) for i in range(lax.axis_size(axis))])  8.1 us
    ppermute x1, starting transfers between devices, from_partner(): return lax.ppermute(x, ALL_AXES, pairs)  5.03 us
    broadcast_in_dim x5, local copies, waits for them, and re-layouts, gathered(): jnp.broadcast_to(x[None], (peers,) + x.shape)  3.51 us
  transfers between devices with their start and end apart: 8, of which 5 were waited for; matrix products, arithmetic and copies ran while one was open for 15% of the time, Pallas kernels for 0%

profile of v2, /device:TPU:1, one launch (start us, length us, event | category | flops | bytes accessed | tf_op | source)
XLA Modules:
  0.0 105.7 jit_solution(4080499611721510305)
XLA Ops:
  0.6 0.7 sqrt.3
  1.3 1.0 multiply_reduce_fusion.1
  2.3 0.7 pad_maximum_fusion
  3.0 0.7 broadcast_in_dim.136
  3.7 5.0 %all-to-all-start.31 = ((bf16[4,40,768]{2,1,0:T(8,128)(2,1)}), bf16[4,40,768]{2,1,0:T(8,128)(2,1)S(1)}, u32[]{:S(2)}, u32[]{:S(2)}) async-start(bf16[4,40,768]{2,1,0:T(8,128)(2,1)} %broadcast_in_dim.136), calls=%async_computation.31 | async-start | bytes 491520 | tf_op jit(solution)/shard_map/all_to_all | solution.py:22
  9.7 4.5 %all-to-all-done.31 = bf16[4,40,768]{2,1,0:T(8,128)(2,1)S(1)} async-done(((bf16[4,40,768]{2,1,0:T(8,128)(2,1)}), bf16[4,40,768]{2,1,0:T(8,128)(2,1)S(1)}, u32[]{:S(2)}, u32[]{:S(2)}) %all-to-all-start.31) | async-done | bytes 245792 | tf_op jit(solution)/shard_map/all_to_all | solution.py:22
  14.2 27.6 %conditional.1 = (bf16[4,40,768]{2,1,0:T(8,128)(2,1)}, bf16[16,32,128]{2,1,0:T(8,128)(2,1)}) conditional(s32[]{:T(128)} %bitcast, (bf16[4,40,768]{2,1,0:T(8,128)(2,1)S(1)}, bf16[32,128]{1,0:T(8,128)(2,1)S(1)}) %tuple.164, (bf16[4,40,768]{2,1,0:T(8,128)(2,1)S(1)}, bf16[32,128]{1,0:T(8,128)(2,1)S(1)}) %tuple.164, ...), branch_computations={%region_0.1_spmd, %region_1.2_spmd, %region_2.3_spmd, %region_3.4_... | conditional | bytes 1515608 | solution.py:75
  14.3 5.0 %collective-permute-start.9 = (bf16[4,40,768]{2,1,0:T(8,128)(2,1)S(1)}, bf16[4,40,768]{2,1,0:T(8,128)(2,1)}, u32[]{:S(2)}, u32[]{:S(2)}) collective-permute-start(bf16[4,40,768]{2,1,0:T(8,128)(2,1)S(1)} %get-tuple-element.144), channel_id=1, source_target_pairs={{80,0},{433,1},{86,2},{439,3},{84,4},{437,5},{82,6},{435,7},{440,8... | collective-permute-start | bytes 737288 | tf_op jit(solution)/shard_map/cond/branch_9_fun/ppermute | solution.py:35
  19.3 0.7 broadcast_in_dim.81
  20.0 12.6 %all-to-all-start.9 = ((bf16[16,32,128]{2,1,0:T(8,128)(2,1)}), bf16[16,32,128]{2,1,0:T(8,128)(2,1)}, u32[]{:S(2)}, u32[]{:S(2)}) async-start(bf16[16,32,128]{2,1,0:T(8,128)(2,1)} %broadcast_in_dim.81), calls=%async_computation.9 | async-start | bytes 262144 | tf_op jit(solution)/shard_map/cond/branch_9_fun/all_to_all | solution.py:22
  32.5 9.3 %all-to-all-done.9 = bf16[16,32,128]{2,1,0:T(8,128)(2,1)} async-done(((bf16[16,32,128]{2,1,0:T(8,128)(2,1)}), bf16[16,32,128]{2,1,0:T(8,128)(2,1)}, u32[]{:S(2)}, u32[]{:S(2)}) %all-to-all-start.9) | async-done | bytes 131104 | tf_op jit(solution)/shard_map/cond/branch_9_fun/all_to_all | solution.py:22
  41.8 0.9 multiply_reduce_fusion.2
  42.8 0.9 reduce_sum.313
  43.7 0.7 broadcast_in_dim.137
  44.5 7.7 %all-to-all-start.32 = ((bf16[32,32,128]{2,1,0:T(8,128)(2,1)}), bf16[32,32,128]{2,1,0:T(8,128)(2,1)S(1)}, u32[]{:S(2)}, u32[]{:S(2)}) async-start(bf16[32,32,128]{2,1,0:T(8,128)(2,1)} %broadcast_in_dim.137), calls=%async_computation.32 | async-start | bytes 524288 | tf_op jit(solution)/shard_map/all_to_all | solution.py:22
  52.2 3.5 %fusion.1 = f32[8,3072]{1,0:T(8,128)S(1)} fusion(bf16[32,3072]{1,0:T(8,128)(2,1)S(1)} %bitcast.66, f32[3072]{0:T(1024)S(1)} %add.129, f32[768]{0:T(1024)S(1)} %get-tuple-element.198, bf16[4,40,768]{2,1,0:T(8,128)(2,1)} %get-tuple-element.193), kind=kOutput, calls=%fused_computation.8 | convolution fusion | flops 200540160 | bytes 371712 | tf_op jit(solution)/shard_map/dot_general | solution.py:92
  55.7 3.5 %convolution_add_fusion.2 = f32[8,3072]{1,0:T(8,128)S(1)} fusion(f32[8,3072]{1,0:T(8,128)S(1)} %fusion.1, bf16[32,3072]{1,0:T(8,128)(2,1)S(1)} %bitcast.67, f32[768]{0:T(1024)S(1)} %get-tuple-element.197, f32[3072]{0:T(1024)S(1)} %add.129, bf16[4,40,768]{2,1,0:T(8,128)(2,1)} %get-tuple-element.193), kind=kOutput, calls=%fused_computation.7 | convolution fusion | flops 200564736 | bytes 470016 | tf_op jit(solution)/shard_map/dot_general | solution.py:92
  59.1 3.5 %convolution_add_fusion.1 = f32[8,3072]{1,0:T(8,128)S(1)} fusion(f32[8,3072]{1,0:T(8,128)S(1)} %convolution_add_fusion.2, bf16[32,3072]{1,0:T(8,128)(2,1)S(1)} %bitcast.68, f32[768]{0:T(1024)S(1)} %get-tuple-element.196, f32[3072]{0:T(1024)S(1)} %add.129, bf16[4,40,768]{2,1,0:T(8,128)(2,1)} %get-tuple-element.193), kind=kOutput, calls=%fused_computation.6 | convolution fusion | flops 200564736 | bytes 470016 | tf_op jit(solution)/shard_map/dot_general | solution.py:92
  62.6 3.6 %fusion.16 = (f32[8]{0:T(128)S(1)}, f32[8,3072]{1,0:T(8,128)S(1)}) fusion(bf16[8,3072]{1,0:T(8,128)(2,1)S(1)} %bitcast.74, f32[8,3072]{1,0:T(8,128)S(1)} %convolution_add_fusion.1, bf16[32,3072]{1,0:T(8,128)(2,1)S(1)} %bitcast.69, f32[768]{0:T(1024)S(1)} %get-tuple-element.195, f32[3072]{0:T(1024)S(1)} %add.129, bf16[4,40,768]{2,1,0:T(8,128)(2,1)} %get-tuple-element.193), kind=kOutput, calls=%fused_computation.28 | convolution fusion | flops 200663040 | bytes 519200 | tf_op jit(solution)/shard_map/dot_general | solution.py:92
  66.3 0.6 copy-done
  67.4 0.7 broadcast_in_dim.143
  68.0 4.2 %all-to-all-start.33 = ((f32[16,8,256]{2,1,0:T(8,128)}), f32[16,8,256]{2,1,0:T(8,128)S(1)}, u32[]{:S(2)}, u32[]{:S(2)}) async-start(f32[16,8,256]{2,1,0:T(8,128)} %broadcast_in_dim.143), calls=%async_computation.33 | async-start | bytes 262144 | tf_op jit(solution)/shard_map/all_to_all | solution.py:22
  72.3 5.0 %collective-permute-start.31 = (f32[8,1536]{1,0:T(8,128)S(1)}, f32[8,1536]{1,0:T(8,128)S(1)}, u32[]{:S(2)}, u32[]{:S(2)}) collective-permute-start(f32[8,1536]{1,0:T(8,128)S(1)} %dynamic-slice_bitcast_fusion), channel_id=1, source_target_pairs={{0,2},{1,3},{2,0},{3,1},{4,6},{5,7},{6,4},{7,5},{8,10},{9,11},{10,... | collective-permute-start | bytes 147464 | tf_op jit(solution)/shard_map/ppermute | solution.py:17
  77.3 4.2 %all-to-all-done.33 = f32[16,8,256]{2,1,0:T(8,128)S(1)} async-done(((f32[16,8,256]{2,1,0:T(8,128)}), f32[16,8,256]{2,1,0:T(8,128)S(1)}, u32[]{:S(2)}, u32[]{:S(2)}) %all-to-all-start.33) | async-done | bytes 131104 | tf_op jit(solution)/shard_map/all_to_all | solution.py:22
  81.5 0.7 broadcast_in_dim.144
  82.2 9.5 %all-to-all-start.34 = ((f32[32,8,256]{2,1,0:T(8,128)}), f32[32,8,256]{2,1,0:T(8,128)S(1)}, u32[]{:S(2)}, u32[]{:S(2)}) async-start(f32[32,8,256]{2,1,0:T(8,128)} %broadcast_in_dim.144), calls=%async_computation.34 | async-start | bytes 524288 | tf_op jit(solution)/shard_map/all_to_all | solution.py:22
  91.7 3.1 %collective-permute-start.32 = (f32[8,768]{1,0:T(8,128)S(1)}, f32[8,768]{1,0:T(8,128)S(1)}, u32[]{:S(2)}, u32[]{:S(2)}) collective-permute-start(f32[8,768]{1,0:T(8,128)S(1)} %dynamic-slice_bitcast_fusion.1), channel_id=1, source_target_pairs={{0,1},{1,0},{2,3},{3,2},{4,5},{5,4},{6,7},{7,6},{8,9},{9,8},{10,11... | collective-permute-start | bytes 73736 | tf_op jit(solution)/shard_map/ppermute | solution.py:17
  94.9 1.7 %collective-permute-done.32 = f32[8,768]{1,0:T(8,128)S(1)} collective-permute-done((f32[8,768]{1,0:T(8,128)S(1)}, f32[8,768]{1,0:T(8,128)S(1)}, u32[]{:S(2)}, u32[]{:S(2)}) %collective-permute-start.32) | collective-permute-done | bytes 24608 | tf_op jit(solution)/shard_map/ppermute | solution.py:17
  96.6 0.6 bitcast_add_fusion.1
  97.2 7.2 %all-to-all-done.34 = f32[32,8,256]{2,1,0:T(8,128)S(1)} async-done(((f32[32,8,256]{2,1,0:T(8,128)}), f32[32,8,256]{2,1,0:T(8,128)S(1)}, u32[]{:S(2)}, u32[]{:S(2)}) %all-to-all-start.34) | async-done | bytes 262176 | tf_op jit(solution)/shard_map/all_to_all | solution.py:22
  104.5 0.6 slice_multiply_fusion.1
  105.1 0.6 fusion.41
  (23 shorter events, 1.1 us)
Async XLA Ops:
  3.7 5.7 %copy-start.1 = (s32[128]{0:T(128)S(1)}, s32[128]{0:T(128)}, u32[]{:S(2)}) copy-start(s32[128]{0:T(128)} %param.40) | copy-start | bytes 1540
  3.7 10.4 %all-to-all-start.31 = ((bf16[4,40,768]{2,1,0:T(8,128)(2,1)}), bf16[4,40,768]{2,1,0:T(8,128)(2,1)S(1)}, u32[]{:S(2)}, u32[]{:S(2)}) async-start(bf16[4,40,768]{2,1,0:T(8,128)(2,1)} %broadcast_in_dim.136), calls=%async_computation.31 | async-start | bytes 491520 | tf_op jit(solution)/shard_map/all_to_all | solution.py:22
  14.3 18.3 %collective-permute-start.9 = (bf16[4,40,768]{2,1,0:T(8,128)(2,1)S(1)}, bf16[4,40,768]{2,1,0:T(8,128)(2,1)}, u32[]{:S(2)}, u32[]{:S(2)}) collective-permute-start(bf16[4,40,768]{2,1,0:T(8,128)(2,1)S(1)} %get-tuple-element.144), channel_id=1, source_target_pairs={{80,0},{433,1},{86,2},{439,3},{84,4},{437,5},{82,6},{435,7},{440,8... | collective-permute-start | bytes 737288 | tf_op jit(solution)/shard_map/cond/branch_9_fun/ppermute | solution.py:35
  20.0 21.9 %all-to-all-start.9 = ((bf16[16,32,128]{2,1,0:T(8,128)(2,1)}), bf16[16,32,128]{2,1,0:T(8,128)(2,1)}, u32[]{:S(2)}, u32[]{:S(2)}) async-start(bf16[16,32,128]{2,1,0:T(8,128)(2,1)} %broadcast_in_dim.81), calls=%async_computation.9 | async-start | bytes 262144 | tf_op jit(solution)/shard_map/cond/branch_9_fun/all_to_all | solution.py:22
  44.5 21.7 %all-to-all-start.32 = ((bf16[32,32,128]{2,1,0:T(8,128)(2,1)}), bf16[32,32,128]{2,1,0:T(8,128)(2,1)S(1)}, u32[]{:S(2)}, u32[]{:S(2)}) async-start(bf16[32,32,128]{2,1,0:T(8,128)(2,1)} %broadcast_in_dim.137), calls=%async_computation.32 | async-start | bytes 524288 | tf_op jit(solution)/shard_map/all_to_all | solution.py:22
  66.2 0.7 copy-start
  68.0 13.4 %all-to-all-start.33 = ((f32[16,8,256]{2,1,0:T(8,128)}), f32[16,8,256]{2,1,0:T(8,128)S(1)}, u32[]{:S(2)}, u32[]{:S(2)}) async-start(f32[16,8,256]{2,1,0:T(8,128)} %broadcast_in_dim.143), calls=%async_computation.33 | async-start | bytes 262144 | tf_op jit(solution)/shard_map/all_to_all | solution.py:22
  72.3 19.4 %collective-permute-start.31 = (f32[8,1536]{1,0:T(8,128)S(1)}, f32[8,1536]{1,0:T(8,128)S(1)}, u32[]{:S(2)}, u32[]{:S(2)}) collective-permute-start(f32[8,1536]{1,0:T(8,128)S(1)} %dynamic-slice_bitcast_fusion), channel_id=1, source_target_pairs={{0,2},{1,3},{2,0},{3,1},{4,6},{5,7},{6,4},{7,5},{8,10},{9,11},{10,... | collective-permute-start | bytes 147464 | tf_op jit(solution)/shard_map/ppermute | solution.py:17
  82.2 22.3 %all-to-all-start.34 = ((f32[32,8,256]{2,1,0:T(8,128)}), f32[32,8,256]{2,1,0:T(8,128)S(1)}, u32[]{:S(2)}, u32[]{:S(2)}) async-start(f32[32,8,256]{2,1,0:T(8,128)} %broadcast_in_dim.144), calls=%async_computation.34 | async-start | bytes 524288 | tf_op jit(solution)/shard_map/all_to_all | solution.py:22
  91.7 4.9 %collective-permute-start.32 = (f32[8,768]{1,0:T(8,128)S(1)}, f32[8,768]{1,0:T(8,128)S(1)}, u32[]{:S(2)}, u32[]{:S(2)}) collective-permute-start(f32[8,768]{1,0:T(8,128)S(1)} %dynamic-slice_bitcast_fusion.1), channel_id=1, source_target_pairs={{0,1},{1,0},{2,3},{3,2},{4,5},{5,4},{6,7},{7,6},{8,9},{9,8},{10,11... | collective-permute-start | bytes 73736 | tf_op jit(solution)/shard_map/ppermute | solution.py:17

commit v3 on v2

v3 whole, which is shorter than its diff:
```python
import functools
import math

import jax
import jax.numpy as jnp
from jax import lax
from jax.experimental import pallas as pl
from jax.experimental.pallas import tpu as pltpu
from jax.sharding import Mesh
from jax.sharding import PartitionSpec as P

Y, ZLO, CORE, ZHI, X = 8, 4, 2, 2, 4
GROUP_AXES = ("y", "zlo", "core")
ALL_AXES = ("y", "zlo", "core", "zhi", "x")
FIRST_SUM, SECOND_SUM = ("y", "core"), ("zlo", "zhi")
MAX_SHIFT = 31
EXTRA = 16
VMEM_LIMIT = 48 * 2**20


def size_of(axes):
    return lax.axis_size(axes)


def exchanged(x, axes):
    return lax.all_to_all(x, axes, 0, 0)


def from_partner(x, shift):
    groups, halves, width = size_of(GROUP_AXES), size_of("zhi"), size_of("x")
    pairs = []
    for group in range(groups):
        for half in range(halves):
            for place in range(width):
                way = 1 - 2 * ((place + group) % 2)
                source = (group + way * shift) % groups
                source = (source * halves + (half ^ place // 2)) * width + place
                pairs.append((source, (group * halves + half) * width + place))
    return lax.ppermute(x, ALL_AXES, pairs)


def local(
    kernel, name, out_shape, *args, scalars=0, flops=0, exps=0, scratch=(), space=pltpu.VMEM, room=VMEM_LIMIT
):
    moved = sum(math.prod(a.shape) * a.dtype.itemsize for a in args)
    specs = [pl.BlockSpec(memory_space=pltpu.SMEM)] * scalars
    specs += [pl.BlockSpec(memory_space=space)] * (len(args) - scalars)
    return pl.pallas_call(
        kernel,
        name=name,
        out_shape=out_shape,
        in_specs=specs,
        out_specs=jax.tree.map(lambda _: pl.BlockSpec(memory_space=pltpu.VMEM), out_shape),
        scratch_shapes=scratch,
        cost_estimate=pl.CostEstimate(flops=flops, bytes_accessed=moved, transcendentals=exps),
        compiler_params=pltpu.CompilerParams(vmem_limit_bytes=room),
    )(*args)


def extended(feat, ones_first):
    wide = feat.astype(jnp.float32)
    half = -0.5 * jnp.sum(wide * wide, axis=0, keepdims=True)
    high = half.astype(jnp.bfloat16).astype(jnp.float32)
    middle = (half - high).astype(jnp.bfloat16).astype(jnp.float32)
    low = half - high - middle
    row = lax.broadcasted_iota(jnp.int32, (EXTRA, feat.shape[1]), 0)
    ones, norm = (0, 3) if ones_first else (3, 0)
    rest = jnp.where((row >= ones) & (row < ones + 3), 1.0, 0.0)
    for offset, piece in enumerate((high, middle, low)):
        rest = jnp.where(row == norm + offset, piece, rest)
    return jnp.concatenate([feat, rest.astype(jnp.bfloat16)], axis=0)


def turned(x):
    return x.astype(jnp.float32).T.astype(jnp.bfloat16)


def prepare_kernel(feat_hbm, scale_hbm, probe_hbm, out_ref, feat_ref, scale_ref, probe_ref, done):
    copies = [
        pltpu.make_async_copy(source, target, done.at[index])
        for index, (source, target) in enumerate(
            ((feat_hbm, feat_ref), (scale_hbm, scale_ref), (probe_hbm, probe_ref))
        )
    ]
    for copy in copies:
        copy.start()
    for copy in copies:
        copy.wait()
    count = feat_ref.shape[0]
    row = lax.broadcasted_iota(jnp.int32, (count, count), 0)
    col = lax.broadcasted_iota(jnp.int32, (count, count), 1)
    spread = jnp.broadcast_to(scale_ref[...], (count, count))
    scale = jnp.sum(jnp.where(row == col, spread, 0.0), axis=1, keepdims=True)
    scaled = (feat_ref[...] * jnp.sqrt(scale)).astype(jnp.bfloat16)
    packed = jnp.concatenate([scaled, probe_ref[...]], axis=0)
    for copy in range(out_ref.shape[0]):
        out_ref[copy] = packed


def own_pivots_kernel(first_ref, packed_ref, pivot_ref, out_ref):
    count, rank = out_ref.shape
    points = packed_ref.shape[2]
    point = lax.broadcasted_iota(jnp.int32, (points, rank), 0) + first_ref[0]
    mask = jnp.where(point == pivot_ref[...], 1.0, 0.0).astype(jnp.bfloat16)
    part = jnp.dot(packed_ref[0, :count], mask, preferred_element_type=jnp.float32)
    out_ref[...] = part.astype(jnp.bfloat16)


def sum_spread_kernel(in_ref, out_ref):
    total = in_ref[0].astype(jnp.float32)
    for peer in range(1, in_ref.shape[0]):
        total = total + in_ref[peer].astype(jnp.float32)
    for copy in range(out_ref.shape[0]):
        out_ref[copy] = total.astype(out_ref.dtype)


def product_kernel(row_ref, col_ref, sum_ref, quad_ref, row_all, col_all, *, count, scale):
    width, probes = row_ref.shape[0], sum_ref.shape[1]
    for place in range(width):
        row_all[place] = extended(row_ref[place, :count], True)
        col_all[place] = turned(extended(col_ref[place, :count], False))

    def step(place, quad):
        total = jnp.zeros(sum_ref.shape[1:], jnp.float32)
        for other in range(width):
            power = jnp.dot(col_all[other], row_all[place], preferred_element_type=jnp.float32)
            kernel = jnp.exp(power).astype(jnp.bfloat16)
            col_probe = col_ref[other, count : count + probes]
            total = total + jnp.dot(col_probe, kernel, preferred_element_type=jnp.float32)
        total = scale * total
        sum_ref[place] = total
        row_probe = row_ref[place, count : count + probes].astype(jnp.float32)
        return quad + jnp.sum(row_probe * total, axis=1, keepdims=True)

    quad = lax.fori_loop(0, width, step, jnp.zeros((probes, 1), jnp.float32))
    quad_ref[...] = jnp.broadcast_to(quad, quad_ref.shape)


def projection_kernel(pivot_ref, here_ref, row_ref, sum_ref, quad_ref, out_ref, *, count):
    width, probes, points = sum_ref.shape
    rank = pivot_ref.shape[2]
    pivot = pivot_ref[0].astype(jnp.float32)
    for peer in range(1, pivot_ref.shape[0]):
        pivot = pivot + pivot_ref[peer].astype(jnp.float32)
    pivot = turned(extended(pivot.astype(jnp.bfloat16), False))
    total = jnp.zeros((probes, rank), jnp.float32)
    for place in range(width):
        row = extended(row_ref[place, :count], True)
        power = jnp.dot(pivot, row, preferred_element_type=jnp.float32)
        kernel = jnp.exp(power).astype(jnp.bfloat16)
        total = total + lax.dot_general(
            row_ref[place, count : count + probes],
            kernel,
            (((1,), (1,)), ((), ())),
            preferred_element_type=jnp.float32,
        )
    total = jnp.where(here_ref[...] != 0, total, 0.0)
    for place in range(width):
        out_ref[place, :, :points] = sum_ref[place]
        out_ref[place, :, points : points + rank] = total
        out_ref[place, :, points + rank :] = quad_ref[...]


def own_sums_kernel(in_ref, product_ref, out_ref):
    probes, points = product_ref.shape
    total = in_ref[0]
    for peer in range(1, in_ref.shape[0]):
        total = total + in_ref[peer]
    product_ref[...] = total[:, :points]
    rank = (total.shape[1] - points) // 2
    rows = [total[probe : probe + 1, points : points + rank] for probe in range(probes)]
    row = lax.broadcasted_iota(jnp.int32, (probes, rank), 0)
    lane = lax.broadcasted_iota(jnp.int32, (probes, rank), 1)
    last = jnp.where(row == lane, total[:, points + rank :], 0.0)
    rows.append(jnp.sum(last, axis=0, keepdims=True))
    packed = jnp.concatenate(rows, axis=1)
    for copy in range(out_ref.shape[0]):
        out_ref[copy] = packed


def body(features, probes, inverse_scales, round_index, pivots):
    count, row_count = features.shape
    probe_count, rank = probes.shape[0], pivots.shape[0]
    rows = count + probe_count
    width = size_of("x")
    block_points = row_count * size_of(("zhi", "x"))
    total_points = block_points * size_of(GROUP_AXES)
    shape = jax.ShapeDtypeStruct

    packed = local(
        prepare_kernel,
        "prepare",
        shape((width, rows, row_count), jnp.bfloat16),
        features,
        inverse_scales.reshape(1, count),
        probes,
        scratch=(
            pltpu.VMEM(features.shape, features.dtype),
            pltpu.VMEM((1, count), inverse_scales.dtype),
            pltpu.VMEM(probes.shape, probes.dtype),
            pltpu.SemaphoreType.DMA((3,)),
        ),
        space=pltpu.HBM,
        room=60 * 2**20,
    )
    quad = exchanged(packed, "x")

    first_point = (lax.axis_index(ALL_AXES) * row_count).astype(jnp.int32)
    pivot_row = pivots.reshape(1, rank)
    pivot_part = local(
        own_pivots_kernel,
        "own_pivots",
        shape((count, rank), jnp.bfloat16),
        first_point.reshape(1),
        packed,
        pivot_row,
        scalars=1,
        flops=2 * count * row_count * rank,
    )
    pivot_here = (pivot_row // row_count % width == lax.axis_index("x")).astype(jnp.int32)

    def fetch(shift):
        def branch(data, part):
            spread = jnp.broadcast_to(part[None], (size_of(FIRST_SUM),) + part.shape)
            some = jnp.sum(exchanged(spread, FIRST_SUM), axis=0)
            pieces = lax.optimization_barrier(from_partner(data, shift))
            return pieces, some

        return branch

    pieces, pivot_some = lax.switch(
        round_index[0] - 1, [fetch(k) for k in range(1, MAX_SHIFT + 1)], quad, pivot_part
    )
    spread = jnp.broadcast_to(pivot_some[None], (size_of(SECOND_SUM), count, rank))
    pivot_all = exchanged(spread, SECOND_SUM)

    sums, quadratic_part = local(
        functools.partial(
            product_kernel, count=count, scale=8.0 / math.sqrt(block_points)
        ),
        "products",
        (
            shape((width, probe_count, row_count), jnp.float32),
            shape((probe_count, rank), jnp.float32),
        ),
        quad,
        pieces,
        flops=2 * (width * row_count) ** 2 * (count + EXTRA + probe_count),
        exps=(width * row_count) ** 2,
        scratch=(
            pltpu.VMEM((width, count + EXTRA, row_count), jnp.bfloat16),
            pltpu.VMEM((width, row_count, count + EXTRA), jnp.bfloat16),
        ),
    )
    parts = local(
        functools.partial(projection_kernel, count=count),
        "projection",
        shape((width, probe_count, row_count + 2 * rank), jnp.float32),
        pivot_all,
        pivot_here,
        quad,
        sums,
        quadratic_part,
        flops=2 * width * row_count * rank * (count + EXTRA + probe_count),
        exps=width * row_count * rank,
    )

    packed_sums = (probe_count + 1) * rank
    product, spread = local(
        own_sums_kernel,
        "own_sums",
        (
            shape((probe_count, row_count), jnp.float32),
            shape((size_of(FIRST_SUM), 1, packed_sums), jnp.float32),
        ),
        exchanged(parts, "x"),
    )
    spread = local(
        sum_spread_kernel,
        "first_sum",
        shape((size_of(SECOND_SUM), 1, packed_sums), jnp.float32),
        exchanged(spread, FIRST_SUM),
    )
    total = jnp.sum(exchanged(spread, SECOND_SUM), axis=(0, 1)) / math.sqrt(total_points)
    projection = 8.0 * total[: probe_count * rank].reshape(probe_count, rank)
    quadratic = total[probe_count * rank : probe_count * rank + probe_count]
    return product, projection, quadratic


def solution(mesh):
    fine = Mesh(mesh.devices.reshape(Y, ZLO, CORE, ZHI, X), ALL_AXES)
    split = P(None, ALL_AXES)
    return jax.shard_map(
        body,
        mesh=fine,
        in_specs=(split, split, P(), P(), P()),
        out_specs=(split, P(), P()),
        check_vma=False,
    )
```

time: 107 us -> 99.5 us (0.930)
  blocking collectives: 0 us -> 39.4 us
  starting transfers between devices: 52.1 us -> 28 us
  matrix products: 14.7 us -> 0 us
  waiting for transfers between devices: 26.9 us -> 13.2 us
  Pallas kernels: 0 us -> 13 us
  other arithmetic: 5.62 us -> 1.58 us
  local copies, waits for them, and re-layouts: 4.92 us -> 2.46 us
    all_to_all x0 -> x3, blocking collectives: none -> 39.4 us  [exchanged(): return lax.all_to_all(x, axes, 0, 0)]
    all_to_all x5 -> x3, starting transfers between devices: 38.9 us -> 22.8 us  [exchanged(): return lax.all_to_all(x, axes, 0, 0)]
    dot_general x6 -> x0, matrix products: 14.7 us -> none  [the longest x4 14 us: body(): jnp.dot(col_probe, kernel, preferred_element_type=jnp.float32)]
    pallas_call x0 -> x6, Pallas kernels: none -> 13 us  [local(): pl.pallas_call(kernel, name=name, out_shape=out_shape, in_specs=specs, ou...]
    all_to_all x5 -> x3, waiting for transfers between devices: 25.2 us -> 12.2 us  [exchanged(): return lax.all_to_all(x, axes, 0, 0)]
    ppermute x2 -> x0, starting transfers between devices: 8.1 us -> none  [crossed(): lax.ppermute(x, axis, [(i, i ^ bit) for i in range(lax.axis_size(axis))])]
    broadcast_in_dim x6 -> x2, local copies, waits for them, and re-layouts: 3.58 us -> 1.3 us  [the longest x1 0.67 us: branch(): spread = jnp.broadcast_to(part[None], (size_of(FIRST_SUM),) + part.shape)]
    reduce_sum x8 -> x2, other arithmetic: 3.05 us -> 0.96 us  [the longest x1 0.93 us: branch(): some = jnp.sum(exchanged(spread, FIRST_SUM), axis=0)]
  transfers between devices with their start and end apart: 8 -> 4, of which waited for: 5 -> 3; matrix products, arithmetic and copies ran while one was open for 15% -> 1% of each run, Pallas kernels for 0% -> 10%
where the time goes in v3:
time: 99.5 us; the launch traced here: 99 us
  blocking collectives  39.4 us (40%)
  starting transfers between devices  28 us (28%)
  waiting for transfers between devices  13.2 us (13%)
  Pallas kernels  13 us (13%)
  local copies, waits for them, and re-layouts  2.46 us (2%)
  other arithmetic  1.58 us (2%)
  between operations  1.35 us (1%)
    all_to_all x3, blocking collectives, exchanged(): return lax.all_to_all(x, axes, 0, 0)  39.4 us
    all_to_all x3, starting transfers between devices, exchanged(): return lax.all_to_all(x, axes, 0, 0)  22.8 us
    pallas_call x6, Pallas kernels, local(): pl.pallas_call(kernel, name=name, out_shape=out_shape, in_specs=specs, ou...  13 us
    all_to_all x3, waiting for transfers between devices, exchanged(): return lax.all_to_all(x, axes, 0, 0)  12.2 us
    ppermute x1, starting transfers between devices, from_partner(): return lax.ppermute(x, ALL_AXES, pairs)  5.24 us
  transfers between devices with their start and end apart: 4, of which 3 were waited for; matrix products, arithmetic and copies ran while one was open for 1% of the time, Pallas kernels for 10%

profile of v3, /device:TPU:1, one launch (start us, length us, event | category | flops | bytes accessed | tf_op | source)
XLA Modules:
  0.0 99.0 jit_solution(13004488849012364540)
XLA Ops:
  0.6 1.7 %prepare.1.packed_ref = bf16[4,40,768]{2,1,0:T(8,128)(2,1)} custom-call(f32[32,768]{1,0:T(8,128)} %feat_hbm.1, f32[1,32]{1,0:T(1,128)} %bitcast.9, bf16[8,768]{1,0:T(8,128)(2,1)} %probe_hbm.1), custom_call_target="tpu_custom_call" | custom-call | bytes 110720 | tf_op jit(solution)/shard_map/prepare/pallas_call | solution.py:48
  2.4 0.0 copy-start
  2.4 5.0 %all-to-all-start.31 = ((bf16[4,40,768]{2,1,0:T(8,128)(2,1)}), bf16[4,40,768]{2,1,0:T(8,128)(2,1)S(1)}, u32[]{:S(2)}, u32[]{:S(2)}) async-start(bf16[4,40,768]{2,1,0:T(8,128)(2,1)} %prepare.1.packed_ref), calls=%async_computation.31 | async-start | bytes 491520 | tf_op jit(solution)/shard_map/all_to_all | solution.py:26
  8.0 0.0 copy-start.1
  8.0 0.0 copy-done
  8.0 0.6 copy-done.1
  8.7 0.2 own_pivots.1
  8.8 4.0 %all-to-all-done.31.row_ref = bf16[4,40,768]{2,1,0:T(8,128)(2,1)S(1)} async-done(((bf16[4,40,768]{2,1,0:T(8,128)(2,1)}), bf16[4,40,768]{2,1,0:T(8,128)(2,1)S(1)}, u32[]{:S(2)}, u32[]{:S(2)}) %all-to-all-start.31) | async-done | bytes 245792 | tf_op jit(solution)/shard_map/all_to_all | solution.py:26
  12.8 23.5 %conditional.1 = (bf16[4,40,768]{2,1,0:T(8,128)(2,1)}, bf16[16,32,128]{2,1,0:T(8,128)(2,1)}) conditional(s32[]{:T(128)} %bitcast, (bf16[4,40,768]{2,1,0:T(8,128)(2,1)S(1)}, bf16[32,128]{1,0:T(8,128)(2,1)S(1)}) %tuple.164, (bf16[4,40,768]{2,1,0:T(8,128)(2,1)S(1)}, bf16[32,128]{1,0:T(8,128)(2,1)S(1)}) %tuple.164, ...), branch_computations={%region_0.1_spmd, %region_1.2_spmd, %region_2.3_spmd, %region_3.4_... | conditional | bytes 1515608 | solution.py:231
  12.8 5.2 %collective-permute-start.23 = (bf16[4,40,768]{2,1,0:T(8,128)(2,1)S(1)}, bf16[4,40,768]{2,1,0:T(8,128)(2,1)}, u32[]{:S(2)}, u32[]{:S(2)}) collective-permute-start(bf16[4,40,768]{2,1,0:T(8,128)(2,1)S(1)} %get-tuple-element.172), channel_id=1, source_target_pairs={{192,0},{321,1},{198,2},{327,3},{196,4},{325,5},{194,6},{323,7},{3... | collective-permute-start | bytes 737288 | tf_op jit(solution)/shard_map/cond/branch_23_fun/ppermute | solution.py:39
  18.0 0.7 broadcast_in_dim.107
  18.7 8.3 %all-to-all-start.23 = ((bf16[16,32,128]{2,1,0:T(8,128)(2,1)}), bf16[16,32,128]{2,1,0:T(8,128)(2,1)}, u32[]{:S(2)}, u32[]{:S(2)}) async-start(bf16[16,32,128]{2,1,0:T(8,128)(2,1)} %broadcast_in_dim.107), calls=%async_computation.23 | async-start | bytes 262144 | tf_op jit(solution)/shard_map/cond/branch_23_fun/all_to_all | solution.py:26
  27.0 1.0 %collective-permute-done.23 = bf16[4,40,768]{2,1,0:T(8,128)(2,1)} collective-permute-done((bf16[4,40,768]{2,1,0:T(8,128)(2,1)S(1)}, bf16[4,40,768]{2,1,0:T(8,128)(2,1)}, u32[]{:S(2)}, u32[]{:S(2)}) %collective-permute-start.23) | collective-permute-done | bytes 245792 | tf_op jit(solution)/shard_map/cond/branch_23_fun/ppermute | solution.py:39
  28.1 8.3 %all-to-all-done.23 = bf16[16,32,128]{2,1,0:T(8,128)(2,1)} async-done(((bf16[16,32,128]{2,1,0:T(8,128)(2,1)}), bf16[16,32,128]{2,1,0:T(8,128)(2,1)}, u32[]{:S(2)}, u32[]{:S(2)}) %all-to-all-start.23) | async-done | bytes 131104 | tf_op jit(solution)/shard_map/cond/branch_23_fun/all_to_all | solution.py:26
  36.3 0.9 reduce_sum.206
  37.2 0.6 broadcast_in_dim.128
  37.9 9.5 %all-to-all-start.32 = ((bf16[8,32,128]{2,1,0:T(8,128)(2,1)}), bf16[8,32,128]{2,1,0:T(8,128)(2,1)S(1)}, u32[]{:S(2)}, u32[]{:S(2)}) async-start(bf16[8,32,128]{2,1,0:T(8,128)(2,1)} %broadcast_in_dim.128), calls=%async_computation.32 | async-start | bytes 131072 | tf_op jit(solution)/shard_map/all_to_all | solution.py:26
  47.4 9.6 %products.1 = (f32[4,8,768]{2,1,0:T(8,128)S(1)}, f32[8,128]{1,0:T(8,128)S(1)}) custom-call(bf16[4,40,768]{2,1,0:T(8,128)(2,1)S(1)} %all-to-all-done.31.row_ref, bf16[4,40,768]{2,1,0:T(8,128)(2,1)} %get-tuple-element.198.col_ref), custom_call_target="tpu_custom_call" | custom-call | flops 1056964608 | bytes 491520 | tf_op jit(solution)/shard_map/products/pallas_call | solution.py:48
  57.0 0.0 all-to-all-done.32.pivot_ref
  57.0 0.8 projection.1
  57.8 10.6 %all_to_all.149.in_ref = f32[4,8,1024]{2,1,0:T(8,128)S(1)} all-to-all(f32[4,8,1024]{2,1,0:T(8,128)S(1)} %projection.1), channel_id=1, replica_groups=mesh['y'=8,'zlo'=4,'core'=2,'zhi'=2,'x'=4] {'x'}, dimensions={0} | all-to-all | bytes 262144 | tf_op jit(solution)/shard_map/all_to_all | solution.py:26
  68.4 0.6 own_sums.1
  69.0 15.4 %all_to_all.150.in_ref = f32[16,1,1152]{2,1,0:T(1,128)S(1)} all-to-all(f32[16,1,1152]{2,1,0:T(1,128)S(1)} %get-tuple-element.202), channel_id=1, replica_groups=mesh['y'=8,'zlo'=4,'core'=2,'zhi'=2,'x'=4] {'y','core'}, dimensions={0} | all-to-all | bytes 147456 | tf_op jit(solution)/shard_map/all_to_all | solution.py:26
  84.4 13.4 %all_to_all.151 = f32[8,1,1152]{2,1,0:T(1,128)S(1)} all-to-all(f32[8,1,1152]{2,1,0:T(1,128)S(1)} %first_sum.1), channel_id=1, replica_groups=mesh['y'=8,'zlo'=4,'core'=2,'zhi'=2,'x'=4] {'zlo','zhi'}, dimensions={0} | all-to-all | bytes 73728 | tf_op jit(solution)/shard_map/all_to_all | solution.py:26
  97.9 0.5 slice.11
  98.4 0.6 fusion
  (4 shorter events, 0.1 us)
Async XLA Ops:
  2.4 5.7 %copy-start = (bf16[4,40,768]{2,1,0:T(8,128)(2,1)S(1)}, bf16[4,40,768]{2,1,0:T(8,128)(2,1)}, u32[]{:S(2)}) copy-start(bf16[4,40,768]{2,1,0:T(8,128)(2,1)} %prepare.1.packed_ref) | copy-start | bytes 737284
  2.4 10.4 %all-to-all-start.31 = ((bf16[4,40,768]{2,1,0:T(8,128)(2,1)}), bf16[4,40,768]{2,1,0:T(8,128)(2,1)S(1)}, u32[]{:S(2)}, u32[]{:S(2)}) async-start(bf16[4,40,768]{2,1,0:T(8,128)(2,1)} %prepare.1.packed_ref), calls=%async_computation.31 | async-start | bytes 491520 | tf_op jit(solution)/shard_map/all_to_all | solution.py:26
  8.0 0.7 copy-start.1
  12.8 15.3 %collective-permute-start.23 = (bf16[4,40,768]{2,1,0:T(8,128)(2,1)S(1)}, bf16[4,40,768]{2,1,0:T(8,128)(2,1)}, u32[]{:S(2)}, u32[]{:S(2)}) collective-permute-start(bf16[4,40,768]{2,1,0:T(8,128)(2,1)S(1)} %get-tuple-element.172), channel_id=1, source_target_pairs={{192,0},{321,1},{198,2},{327,3},{196,4},{325,5},{194,6},{323,7},{3... | collective-permute-start | bytes 737288 | tf_op jit(solution)/shard_map/cond/branch_23_fun/ppermute | solution.py:39
  18.7 17.6 %all-to-all-start.23 = ((bf16[16,32,128]{2,1,0:T(8,128)(2,1)}), bf16[16,32,128]{2,1,0:T(8,128)(2,1)}, u32[]{:S(2)}, u32[]{:S(2)}) async-start(bf16[16,32,128]{2,1,0:T(8,128)(2,1)} %broadcast_in_dim.107), calls=%async_computation.23 | async-start | bytes 262144 | tf_op jit(solution)/shard_map/cond/branch_23_fun/all_to_all | solution.py:26
  37.9 19.1 %all-to-all-start.32 = ((bf16[8,32,128]{2,1,0:T(8,128)(2,1)}), bf16[8,32,128]{2,1,0:T(8,128)(2,1)S(1)}, u32[]{:S(2)}, u32[]{:S(2)}) async-start(bf16[8,32,128]{2,1,0:T(8,128)(2,1)} %broadcast_in_dim.128), calls=%async_computation.32 | async-start | bytes 131072 | tf_op jit(solution)/shard_map/all_to_all | solution.py:26

commit v4 on v3

--- a/solution.py
+++ b/solution.py
@@ -114,31 +114,60 @@
         out_ref[copy] = total.astype(out_ref.dtype)
 
 
-def product_kernel(row_ref, col_ref, sum_ref, quad_ref, row_all, col_all, *, count, scale):
+def pair_sum(row_all, col_all, col_ref, place, other, count, probes):
+    power = jnp.dot(col_all[other], row_all[place], preferred_element_type=jnp.float32)
+    kernel = jnp.exp(power).astype(jnp.bfloat16)
+    col_probe = col_ref[other, count : count + probes]
+    return jnp.dot(col_probe, kernel, preferred_element_type=jnp.float32)
+
+
+def first_half_kernel(
+    ahead_ref, row_ref, col_ref, sum_ref, quad_ref, row_all, col_all, *, count, scale
+):
     width, probes = row_ref.shape[0], sum_ref.shape[1]
+    ahead = ahead_ref[0] == 1
     for place in range(width):
         row_all[place] = extended(row_ref[place, :count], True)
         col_all[place] = turned(extended(col_ref[place, :count], False))
-
-    def step(place, quad):
-        total = jnp.zeros(sum_ref.shape[1:], jnp.float32)
-        for other in range(width):
-            power = jnp.dot(col_all[other], row_all[place], preferred_element_type=jnp.float32)
-            kernel = jnp.exp(power).astype(jnp.bfloat16)
-            col_probe = col_ref[other, count : count + probes]
-            total = total + jnp.dot(col_probe, kernel, preferred_element_type=jnp.float32)
-        total = scale * total
-        sum_ref[place] = total
+    sum_ref[...] = jnp.zeros_like(sum_ref)
+
+    def step(turn, carry):
+        for part in range(4):
+            place = jnp.where(ahead, 2 * turn + part // 2, 2 + turn)
+            other = jnp.where(ahead, part % 2, part)
+            sum_ref[place] += pair_sum(row_all, col_all, col_ref, place, other, count, probes)
+        return carry
+
+    lax.fori_loop(0, 2, step, 0)
+    quad = jnp.zeros((probes, 1), jnp.float32)
+    for place in range(width):
         row_probe = row_ref[place, count : count + probes].astype(jnp.float32)
-        return quad + jnp.sum(row_probe * total, axis=1, keepdims=True)
-
-    quad = lax.fori_loop(0, width, step, jnp.zeros((probes, 1), jnp.float32))
-    quad_ref[...] = jnp.broadcast_to(quad, quad_ref.shape)
-
-
-def projection_kernel(pivot_ref, here_ref, row_ref, sum_ref, quad_ref, out_ref, *, count):
-    width, probes, points = sum_ref.shape
-    rank = pivot_ref.shape[2]
+        quad = quad + jnp.sum(row_probe * sum_ref[place], axis=1, keepdims=True)
+    quad_ref[...] = jnp.broadcast_to(scale * quad, quad_ref.shape)
+
+
+def second_half_kernel(
+    ahead_ref, row_all, col_all, col_ref, first_ref, sum_ref, *, count, scale
+):
+    width, probes = first_ref.shape[:2]
+    ahead = ahead_ref[0] == 1
+    sum_ref[...] = first_ref[...]
+
+    def step(turn, carry):
+        for part in range(4):
+            place = jnp.where(ahead, 2 * turn + part // 2, turn)
+            other = jnp.where(ahead, 2 + part % 2, part)
+            sum_ref[place] += pair_sum(row_all, col_all, col_ref, place, other, count, probes)
+        return carry
+
+    lax.fori_loop(0, 2, step, 0)
+    for place in range(width):
+        sum_ref[place] = scale * sum_ref[place]
+
+
+def projection_kernel(pivot_ref, here_ref, row_ref, quad_ref, out_ref, *, count):
+    width, rank = row_ref.shape[0], pivot_ref.shape[2]
+    probes = quad_ref.shape[0]
     pivot = pivot_ref[0].astype(jnp.float32)
     for peer in range(1, pivot_ref.shape[0]):
         pivot = pivot + pivot_ref[peer].astype(jnp.float32)
@@ -155,27 +184,38 @@
             preferred_element_type=jnp.float32,
         )
     total = jnp.where(here_ref[...] != 0, total, 0.0)
+    rows = [total[probe : probe + 1] for probe in range(probes)]
+    row = lax.broadcasted_iota(jnp.int32, (probes, rank), 0)
+    lane = lax.broadcasted_iota(jnp.int32, (probes, rank), 1)
+    rows.append(jnp.sum(jnp.where(row == lane, quad_ref[...], 0.0), axis=0, keepdims=True))
+    packed = jnp.concatenate(rows, axis=1)
+    for copy in range(out_ref.shape[0]):
+        out_ref[copy] = packed
+
+
+def join_kernel(sum_ref, total_ref, out_ref):
+    width, probes, points = sum_ref.shape
+    rank = (out_ref.shape[2] - points) // 2
+    total = total_ref[0]
+    for peer in range(1, total_ref.shape[0]):
+        total = total + total_ref[peer]
+    rows = [total[:, probe * rank : (probe + 1) * rank] for probe in range(probes)]
+    last = jnp.broadcast_to(total[:, probes * rank :], (probes, rank))
+    joined = jnp.concatenate([jnp.concatenate(rows, axis=0), last], axis=1)
     for place in range(width):
         out_ref[place, :, :points] = sum_ref[place]
-        out_ref[place, :, points : points + rank] = total
-        out_ref[place, :, points + rank :] = quad_ref[...]
-
-
-def own_sums_kernel(in_ref, product_ref, out_ref):
+        out_ref[place, :, points:] = joined
+
+
+def finish_kernel(in_ref, product_ref, projection_ref, quadratic_ref, *, projection_scale):
     probes, points = product_ref.shape
+    rank = projection_ref.shape[1]
     total = in_ref[0]
     for peer in range(1, in_ref.shape[0]):
         total = total + in_ref[peer]
     product_ref[...] = total[:, :points]
-    rank = (total.shape[1] - points) // 2
-    rows = [total[probe : probe + 1, points : points + rank] for probe in range(probes)]
-    row = lax.broadcasted_iota(jnp.int32, (probes, rank), 0)
-    lane = lax.broadcasted_iota(jnp.int32, (probes, rank), 1)
-    last = jnp.where(row == lane, total[:, points + rank :], 0.0)
-    rows.append(jnp.sum(last, axis=0, keepdims=True))
-    packed = jnp.concatenate(rows, axis=1)
-    for copy in range(out_ref.shape[0]):
-        out_ref[copy] = packed
+    projection_ref[...] = projection_scale * total[:, points : points + rank]
+    quadratic_ref[...] = total[0, points + rank : points + rank + probes]
 
 
 def body(features, probes, inverse_scales, round_index, pivots):
@@ -221,8 +261,8 @@
 
     def fetch(shift):
         def branch(data, part):
-            spread = jnp.broadcast_to(part[None], (size_of(FIRST_SUM),) + part.shape)
-            some = jnp.sum(exchanged(spread, FIRST_SUM), axis=0)
+            spread = jnp.broadcast_to(part[None], (size_of(SECOND_SUM),) + part.shape)
+            some = jnp.sum(exchanged(spread, SECOND_SUM), axis=0)
             pieces = lax.optimization_barrier(from_partner(data, shift))
             return pieces, some
 
@@ -231,59 +271,82 @@
     pieces, pivot_some = lax.switch(
         round_index[0] - 1, [fetch(k) for k in range(1, MAX_SHIFT + 1)], quad, pivot_part
     )
-    spread = jnp.broadcast_to(pivot_some[None], (size_of(SECOND_SUM), count, rank))
-    pivot_all = exchanged(spread, SECOND_SUM)
-
-    sums, quadratic_part = local(
+    spread = jnp.broadcast_to(pivot_some[None], (size_of(FIRST_SUM), count, rank))
+    pivot_all = exchanged(spread, FIRST_SUM)
+
+    product_scale = 8.0 / math.sqrt(block_points)
+    flops = (width * row_count) ** 2 * (count + EXTRA + probe_count)
+    exps = (width * row_count) ** 2 // 2
+    ahead = ((lax.axis_index("x") + lax.axis_index(GROUP_AXES) + 1) % 2).astype(jnp.int32).reshape(1)
+    first, quadratic_part, row_all, col_all = local(
         functools.partial(
-            product_kernel, count=count, scale=8.0 / math.sqrt(block_points)
+            first_half_kernel,
+            count=count,
+            scale=2.0 * product_scale / math.sqrt(total_points),
         ),
-        "products",
+        "first_half",
         (
             shape((width, probe_count, row_count), jnp.float32),
             shape((probe_count, rank), jnp.float32),
+            shape((width, count + EXTRA, row_count), jnp.bfloat16),
+            shape((width, row_count, count + EXTRA), jnp.bfloat16),
         ),
+        ahead,
         quad,
         pieces,
-        flops=2 * (width * row_count) ** 2 * (count + EXTRA + probe_count),
-        exps=(width * row_count) ** 2,
-        scratch=(
-            pltpu.VMEM((width, count + EXTRA, row_count), jnp.bfloat16),
-            pltpu.VMEM((width, row_count, count + EXTRA), jnp.bfloat16),
-        ),
-    )
-    parts = local(
+        scalars=1,
+        flops=flops,
+        exps=exps,
+    )
+    packed_sums = (probe_count + 1) * rank
+    spread = local(
         functools.partial(projection_kernel, count=count),
         "projection",
-        shape((width, probe_count, row_count + 2 * rank), jnp.float32),
+        shape((size_of(FIRST_SUM), 1, packed_sums), jnp.float32),
         pivot_all,
         pivot_here,
         quad,
-        sums,
         quadratic_part,
         flops=2 * width * row_count * rank * (count + EXTRA + probe_count),
         exps=width * row_count * rank,
     )
-
-    packed_sums = (probe_count + 1) * rank
-    product, spread = local(
-        own_sums_kernel,
-        "own_sums",
-        (
-            shape((probe_count, row_count), jnp.float32),
-            shape((size_of(FIRST_SUM), 1, packed_sums), jnp.float32),
-        ),
-        exchanged(parts, "x"),
+    some = exchanged(spread, FIRST_SUM)
+    sums = local(
+        functools.partial(second_half_kernel, count=count, scale=product_scale),
+        "second_half",
+        shape((width, probe_count, row_count), jnp.float32),
+        ahead,
+        row_all,
+        col_all,
+        pieces,
+        first,
+        scalars=1,
+        flops=flops,
+        exps=exps,
     )
     spread = local(
         sum_spread_kernel,
         "first_sum",
         shape((size_of(SECOND_SUM), 1, packed_sums), jnp.float32),
-        exchanged(spread, FIRST_SUM),
-    )
-    total = jnp.sum(exchanged(spread, SECOND_SUM), axis=(0, 1)) / math.sqrt(total_points)
-    projection = 8.0 * total[: probe_count * rank].reshape(probe_count, rank)
-    quadratic = total[probe_count * rank : probe_count * rank + probe_count]
+        some,
+    )
+    parts = local(
+        join_kernel,
+        "join",
+        shape((width, probe_count, row_count + 2 * rank), jnp.float32),
+        sums,
+        exchanged(spread, SECOND_SUM),
+    )
+    product, projection, quadratic = local(
+        functools.partial(finish_kernel, projection_scale=8.0 / math.sqrt(total_points)),
+        "finish",
+        (
+            shape((probe_count, row_count), jnp.float32),
+            shape((probe_count, rank), jnp.float32),
+            shape((probe_count,), jnp.float32),
+        ),
+        exchanged(parts, "x"),
+    )
     return product, projection, quadratic
 
 

time: 99.5 us -> 95.3 us (0.958)
  blocking collectives: 39.4 us -> 22.1 us
  starting transfers between devices: 28 us -> 37.4 us
  waiting for transfers between devices: 13.2 us -> 15.4 us
  Pallas kernels: 13 us -> 15.1 us
    all_to_all x3 -> x2, blocking collectives: 39.4 us -> 22.1 us  [exchanged(): return lax.all_to_all(x, axes, 0, 0)]
    all_to_all x3 -> x4, starting transfers between devices: 22.8 us -> 30.4 us  [exchanged(): return lax.all_to_all(x, axes, 0, 0)]
    pallas_call x6 -> x8, Pallas kernels: 13 us -> 15.1 us  [local(): pl.pallas_call(kernel, name=name, out_shape=out_shape, in_specs=specs, ou...]
    ppermute x1, starting transfers between devices: 5.24 us -> 7.04 us  [from_partner(): return lax.ppermute(x, ALL_AXES, pairs)]
    all_to_all x3 -> x4, waiting for transfers between devices: 12.2 us -> 13.4 us  [exchanged(): return lax.all_to_all(x, axes, 0, 0)]
    ppermute x1, waiting for transfers between devices: 1.02 us -> 2.03 us  [from_partner(): return lax.ppermute(x, ALL_AXES, pairs)]
  transfers between devices with their start and end apart: 4 -> 5, of which waited for: 3 -> 5; matrix products, arithmetic and copies ran while one was open for 1% -> 1% of each run, Pallas kernels for 10% -> 12%
where the time goes in v4:
time: 95.3 us; the launch traced here: 94.2 us
  starting transfers between devices  37.4 us (39%)
  blocking collectives  22.1 us (23%)
  waiting for transfers between devices  15.4 us (16%)
  Pallas kernels  15.1 us (16%)
  local copies, waits for them, and re-layouts  1.96 us (2%)
  between operations  1.35 us (1%)
    all_to_all x4, starting transfers between devices, exchanged(): return lax.all_to_all(x, axes, 0, 0)  30.4 us
    all_to_all x2, blocking collectives, exchanged(): return lax.all_to_all(x, axes, 0, 0)  22.1 us
    pallas_call x8, Pallas kernels, local(): pl.pallas_call(kernel, name=name, out_shape=out_shape, in_specs=specs, ou...  15.1 us
    all_to_all x4, waiting for transfers between devices, exchanged(): return lax.all_to_all(x, axes, 0, 0)  13.4 us
    ppermute x1, starting transfers between devices, from_partner(): return lax.ppermute(x, ALL_AXES, pairs)  7.04 us
    ppermute x1, waiting for transfers between devices, from_partner(): return lax.ppermute(x, ALL_AXES, pairs)  2.03 us
  transfers between devices with their start and end apart: 5, of which 5 were waited for; matrix products, arithmetic and copies ran while one was open for 1% of the time, Pallas kernels for 12%

profile of v4, /device:TPU:1, one launch (start us, length us, event | category | flops | bytes accessed | tf_op | source)
XLA Modules:
  0.0 94.2 jit_solution(16526948146403368896)
XLA Ops:
  0.6 1.7 %prepare.1.packed_ref = bf16[4,40,768]{2,1,0:T(8,128)(2,1)} custom-call(f32[32,768]{1,0:T(8,128)} %feat_hbm.1, f32[1,32]{1,0:T(1,128)} %bitcast.8, bf16[8,768]{1,0:T(8,128)(2,1)} %probe_hbm.1), custom_call_target="tpu_custom_call" | custom-call | bytes 110720 | tf_op jit(solution)/shard_map/prepare/pallas_call | solution.py:48
  2.4 0.0 copy-start
  2.4 5.0 %all-to-all-start.31 = ((bf16[4,40,768]{2,1,0:T(8,128)(2,1)}), bf16[4,40,768]{2,1,0:T(8,128)(2,1)S(1)}, u32[]{:S(2)}, u32[]{:S(2)}) async-start(bf16[4,40,768]{2,1,0:T(8,128)(2,1)} %prepare.1.packed_ref), calls=%async_computation.31 | async-start | bytes 491520 | tf_op jit(solution)/shard_map/all_to_all | solution.py:26
  8.0 0.0 copy-start.1
  8.0 0.0 copy-done
  8.0 0.6 copy-done.1
  8.7 0.2 own_pivots.1
  8.8 4.0 %all-to-all-done.31.row_ref = bf16[4,40,768]{2,1,0:T(8,128)(2,1)S(1)} async-done(((bf16[4,40,768]{2,1,0:T(8,128)(2,1)}), bf16[4,40,768]{2,1,0:T(8,128)(2,1)S(1)}, u32[]{:S(2)}, u32[]{:S(2)}) %all-to-all-start.31) | async-done | bytes 245792 | tf_op jit(solution)/shard_map/all_to_all | solution.py:26
  12.8 24.8 %conditional.1 = (bf16[4,40,768]{2,1,0:T(8,128)(2,1)}, bf16[8,32,128]{2,1,0:T(8,128)(2,1)}) conditional(s32[]{:T(128)} %bitcast.2, (bf16[4,40,768]{2,1,0:T(8,128)(2,1)S(1)}, bf16[32,128]{1,0:T(8,128)(2,1)S(1)}) %tuple.163, (bf16[4,40,768]{2,1,0:T(8,128)(2,1)S(1)}, bf16[32,128]{1,0:T(8,128)(2,1)S(1)}) %tuple.163, ...), branch_computations={%region_0.1_spmd, %region_1.2_spmd, %region_2.3_spmd, %region_3.4_... | conditional | bytes 1253464 | solution.py:271
  12.8 7.0 %collective-permute-start.25 = (bf16[4,40,768]{2,1,0:T(8,128)(2,1)S(1)}, bf16[4,40,768]{2,1,0:T(8,128)(2,1)}, u32[]{:S(2)}, u32[]{:S(2)}) collective-permute-start(bf16[4,40,768]{2,1,0:T(8,128)(2,1)S(1)} %get-tuple-element.176), channel_id=1, source_target_pairs={{208,0},{305,1},{214,2},{311,3},{212,4},{309,5},{210,6},{307,7},{3... | collective-permute-start | bytes 737288 | tf_op jit(solution)/shard_map/cond/branch_25_fun/ppermute | solution.py:39
  19.8 0.6 broadcast_in_dim.113
  20.5 10.4 %all-to-all-start.25 = ((bf16[8,32,128]{2,1,0:T(8,128)(2,1)}), bf16[8,32,128]{2,1,0:T(8,128)(2,1)}, u32[]{:S(2)}, u32[]{:S(2)}) async-start(bf16[8,32,128]{2,1,0:T(8,128)(2,1)} %broadcast_in_dim.113), calls=%async_computation.25 | async-start | bytes 131072 | tf_op jit(solution)/shard_map/cond/branch_25_fun/all_to_all | solution.py:26
  30.9 2.0 %collective-permute-done.25 = bf16[4,40,768]{2,1,0:T(8,128)(2,1)} collective-permute-done((bf16[4,40,768]{2,1,0:T(8,128)(2,1)S(1)}, bf16[4,40,768]{2,1,0:T(8,128)(2,1)}, u32[]{:S(2)}, u32[]{:S(2)}) %collective-permute-start.25) | collective-permute-done | bytes 245792 | tf_op jit(solution)/shard_map/cond/branch_25_fun/ppermute | solution.py:39
  32.9 4.7 %all-to-all-done.25 = bf16[8,32,128]{2,1,0:T(8,128)(2,1)} async-done(((bf16[8,32,128]{2,1,0:T(8,128)(2,1)}), bf16[8,32,128]{2,1,0:T(8,128)(2,1)}, u32[]{:S(2)}, u32[]{:S(2)}) %all-to-all-start.25) | async-done | bytes 65568 | tf_op jit(solution)/shard_map/cond/branch_25_fun/all_to_all | solution.py:26
  37.6 0.9 reduce_sum.194
  38.5 0.7 broadcast_in_dim.128
  39.2 9.8 %all-to-all-start.32 = ((bf16[16,32,128]{2,1,0:T(8,128)(2,1)}), bf16[16,32,128]{2,1,0:T(8,128)(2,1)S(1)}, u32[]{:S(2)}, u32[]{:S(2)}) async-start(bf16[16,32,128]{2,1,0:T(8,128)(2,1)} %broadcast_in_dim.128), calls=%async_computation.32 | async-start | bytes 262144 | tf_op jit(solution)/shard_map/all_to_all | solution.py:26
  49.0 5.8 %first_half.1 = (f32[4,8,768]{2,1,0:T(8,128)S(1)}, f32[8,128]{1,0:T(8,128)S(1)}, bf16[4,48,768]{2,1,0:T(8,128)(2,1)S(1)}, bf16[4,768,48]{2,1,0:T(8,128)(2,1)S(1)}) custom-call(s32[1]{0:T(128)} %bitcast.ahead_ref, bf16[4,40,768]{2,1,0:T(8,128)(2,1)S(1)} %all-to-all-done.31.row_ref, bf16[4,40,768]{2,1,0:T(8,128)(2,1)} %get-tuple-element.197.col_ref), custom_call_target="tpu_custom_call" | custom-call | flops 528482304 | bytes 491524 | tf_op jit(solution)/shard_map/first_half/pallas_call | solution.py:48
  54.8 3.4 %all-to-all-done.32.pivot_ref = bf16[16,32,128]{2,1,0:T(8,128)(2,1)S(1)} async-done(((bf16[16,32,128]{2,1,0:T(8,128)(2,1)}), bf16[16,32,128]{2,1,0:T(8,128)(2,1)S(1)}, u32[]{:S(2)}, u32[]{:S(2)}) %all-to-all-start.32) | async-done | bytes 131104 | tf_op jit(solution)/shard_map/all_to_all | solution.py:26
  58.2 0.8 projection.1
  59.1 11.6 %all_to_all.149.in_ref = f32[16,1,1152]{2,1,0:T(1,128)S(1)} all-to-all(f32[16,1,1152]{2,1,0:T(1,128)S(1)} %projection.1), channel_id=1, replica_groups=mesh['y'=8,'zlo'=4,'core'=2,'zhi'=2,'x'=4] {'y','core'}, dimensions={0} | all-to-all | bytes 147456 | tf_op jit(solution)/shard_map/all_to_all | solution.py:26
  70.7 0.6 first_sum.1
  71.3 5.1 %all-to-all-start.34 = ((f32[8,1,1152]{2,1,0:T(1,128)}), f32[8,1,1152]{2,1,0:T(1,128)S(1)}, u32[]{:S(2)}, u32[]{:S(2)}) async-start(f32[8,1,1152]{2,1,0:T(1,128)} %first_sum.1), calls=%async_computation.34 | async-start | bytes 73728 | tf_op jit(solution)/shard_map/all_to_all | solution.py:26
  76.5 5.4 %second_half.1.sum_ref = f32[4,8,768]{2,1,0:T(8,128)S(1)} custom-call(s32[1]{0:T(128)} %bitcast.ahead_ref, bf16[4,48,768]{2,1,0:T(8,128)(2,1)S(1)} %get-tuple-element.198.row_all, bf16[4,768,48]{2,1,0:T(8,128)(2,1)S(1)} %get-tuple-element.199.col_all, bf16[4,40,768]{2,1,0:T(8,128)(2,1)} %get-tuple-element.197.col_ref, ...), custom_call_target="tpu_custom_call" | custom-call | flops 528482304 | bytes 933892 | tf_op jit(solution)/shard_map/second_half/pallas_call | solution.py:48
  81.8 1.3 %all-to-all-done.34.total_ref = f32[8,1,1152]{2,1,0:T(1,128)S(1)} async-done(((f32[8,1,1152]{2,1,0:T(1,128)}), f32[8,1,1152]{2,1,0:T(1,128)S(1)}, u32[]{:S(2)}, u32[]{:S(2)}) %all-to-all-start.34) | async-done | bytes 36896 | tf_op jit(solution)/shard_map/all_to_all | solution.py:26
  83.1 10.4 %all_to_all.150.in_ref = f32[4,8,1024]{2,1,0:T(8,128)S(1)} all-to-all(f32[4,8,1024]{2,1,0:T(8,128)S(1)} %join.1), channel_id=1, replica_groups=mesh['y'=8,'zlo'=4,'core'=2,'zhi'=2,'x'=4] {'x'}, dimensions={0} | all-to-all | bytes 262144 | tf_op jit(solution)/shard_map/all_to_all | solution.py:26
  93.6 0.6 finish.1
  (2 shorter events, 0.0 us)
Async XLA Ops:
  2.4 5.7 %copy-start = (bf16[4,40,768]{2,1,0:T(8,128)(2,1)S(1)}, bf16[4,40,768]{2,1,0:T(8,128)(2,1)}, u32[]{:S(2)}) copy-start(bf16[4,40,768]{2,1,0:T(8,128)(2,1)} %prepare.1.packed_ref) | copy-start | bytes 737284
  2.4 10.4 %all-to-all-start.31 = ((bf16[4,40,768]{2,1,0:T(8,128)(2,1)}), bf16[4,40,768]{2,1,0:T(8,128)(2,1)S(1)}, u32[]{:S(2)}, u32[]{:S(2)}) async-start(bf16[4,40,768]{2,1,0:T(8,128)(2,1)} %prepare.1.packed_ref), calls=%async_computation.31 | async-start | bytes 491520 | tf_op jit(solution)/shard_map/all_to_all | solution.py:26
  8.0 0.7 copy-start.1
  12.8 20.1 %collective-permute-start.25 = (bf16[4,40,768]{2,1,0:T(8,128)(2,1)S(1)}, bf16[4,40,768]{2,1,0:T(8,128)(2,1)}, u32[]{:S(2)}, u32[]{:S(2)}) collective-permute-start(bf16[4,40,768]{2,1,0:T(8,128)(2,1)S(1)} %get-tuple-element.176), channel_id=1, source_target_pairs={{208,0},{305,1},{214,2},{311,3},{212,4},{309,5},{210,6},{307,7},{3... | collective-permute-start | bytes 737288 | tf_op jit(solution)/shard_map/cond/branch_25_fun/ppermute | solution.py:39
  20.5 17.1 %all-to-all-start.25 = ((bf16[8,32,128]{2,1,0:T(8,128)(2,1)}), bf16[8,32,128]{2,1,0:T(8,128)(2,1)}, u32[]{:S(2)}, u32[]{:S(2)}) async-start(bf16[8,32,128]{2,1,0:T(8,128)(2,1)} %broadcast_in_dim.113), calls=%async_computation.25 | async-start | bytes 131072 | tf_op jit(solution)/shard_map/cond/branch_25_fun/all_to_all | solution.py:26
  39.2 19.0 %all-to-all-start.32 = ((bf16[16,32,128]{2,1,0:T(8,128)(2,1)}), bf16[16,32,128]{2,1,0:T(8,128)(2,1)S(1)}, u32[]{:S(2)}, u32[]{:S(2)}) async-start(bf16[16,32,128]{2,1,0:T(8,128)(2,1)} %broadcast_in_dim.128), calls=%async_computation.32 | async-start | bytes 262144 | tf_op jit(solution)/shard_map/all_to_all | solution.py:26
  71.3 11.8 %all-to-all-start.34 = ((f32[8,1,1152]{2,1,0:T(1,128)}), f32[8,1,1152]{2,1,0:T(1,128)S(1)}, u32[]{:S(2)}, u32[]{:S(2)}) async-start(f32[8,1,1152]{2,1,0:T(1,128)} %first_sum.1), calls=%async_computation.34 | async-start | bytes 73728 | tf_op jit(solution)/shard_map/all_to_all | solution.py:26

commit v5 on v4

--- a/solution.py
+++ b/solution.py
@@ -122,7 +122,18 @@
 
 
 def first_half_kernel(
-    ahead_ref, row_ref, col_ref, sum_ref, quad_ref, row_all, col_all, *, count, scale
+    ahead_ref,
+    row_ref,
+    col_ref,
+    pivot_ref,
+    here_ref,
+    sum_ref,
+    out_ref,
+    row_all,
+    col_all,
+    *,
+    count,
+    scale,
 ):
     width, probes = row_ref.shape[0], sum_ref.shape[1]
     ahead = ahead_ref[0] == 1
@@ -143,39 +154,14 @@
     for place in range(width):
         row_probe = row_ref[place, count : count + probes].astype(jnp.float32)
         quad = quad + jnp.sum(row_probe * sum_ref[place], axis=1, keepdims=True)
-    quad_ref[...] = jnp.broadcast_to(scale * quad, quad_ref.shape)
-
-
-def second_half_kernel(
-    ahead_ref, row_all, col_all, col_ref, first_ref, sum_ref, *, count, scale
-):
-    width, probes = first_ref.shape[:2]
-    ahead = ahead_ref[0] == 1
-    sum_ref[...] = first_ref[...]
-
-    def step(turn, carry):
-        for part in range(4):
-            place = jnp.where(ahead, 2 * turn + part // 2, turn)
-            other = jnp.where(ahead, 2 + part % 2, part)
-            sum_ref[place] += pair_sum(row_all, col_all, col_ref, place, other, count, probes)
-        return carry
-
-    lax.fori_loop(0, 2, step, 0)
-    for place in range(width):
-        sum_ref[place] = scale * sum_ref[place]
-
-
-def projection_kernel(pivot_ref, here_ref, row_ref, quad_ref, out_ref, *, count):
-    width, rank = row_ref.shape[0], pivot_ref.shape[2]
-    probes = quad_ref.shape[0]
+    rank = pivot_ref.shape[2]
     pivot = pivot_ref[0].astype(jnp.float32)
     for peer in range(1, pivot_ref.shape[0]):
         pivot = pivot + pivot_ref[peer].astype(jnp.float32)
     pivot = turned(extended(pivot.astype(jnp.bfloat16), False))
     total = jnp.zeros((probes, rank), jnp.float32)
     for place in range(width):
-        row = extended(row_ref[place, :count], True)
-        power = jnp.dot(pivot, row, preferred_element_type=jnp.float32)
+        power = jnp.dot(pivot, row_all[place], preferred_element_type=jnp.float32)
         kernel = jnp.exp(power).astype(jnp.bfloat16)
         total = total + lax.dot_general(
             row_ref[place, count : count + probes],
@@ -187,10 +173,30 @@
     rows = [total[probe : probe + 1] for probe in range(probes)]
     row = lax.broadcasted_iota(jnp.int32, (probes, rank), 0)
     lane = lax.broadcasted_iota(jnp.int32, (probes, rank), 1)
-    rows.append(jnp.sum(jnp.where(row == lane, quad_ref[...], 0.0), axis=0, keepdims=True))
+    quad = jnp.broadcast_to(scale * quad, (probes, rank))
+    rows.append(jnp.sum(jnp.where(row == lane, quad, 0.0), axis=0, keepdims=True))
     packed = jnp.concatenate(rows, axis=1)
     for copy in range(out_ref.shape[0]):
         out_ref[copy] = packed
+
+
+def second_half_kernel(
+    ahead_ref, row_all, col_all, col_ref, first_ref, sum_ref, *, count, scale
+):
+    width, probes = first_ref.shape[:2]
+    ahead = ahead_ref[0] == 1
+    sum_ref[...] = first_ref[...]
+
+    def step(turn, carry):
+        for part in range(4):
+            place = jnp.where(ahead, 2 * turn + part // 2, turn)
+            other = jnp.where(ahead, 2 + part % 2, part)
+            sum_ref[place] += pair_sum(row_all, col_all, col_ref, place, other, count, probes)
+        return carry
+
+    lax.fori_loop(0, 2, step, 0)
+    for place in range(width):
+        sum_ref[place] = scale * sum_ref[place]
 
 
 def join_kernel(sum_ref, total_ref, out_ref):
@@ -262,23 +268,27 @@
     def fetch(shift):
         def branch(data, part):
             spread = jnp.broadcast_to(part[None], (size_of(SECOND_SUM),) + part.shape)
-            some = jnp.sum(exchanged(spread, SECOND_SUM), axis=0)
-            pieces = lax.optimization_barrier(from_partner(data, shift))
-            return pieces, some
+            some = local(
+                sum_spread_kernel,
+                "pivot_sum",
+                shape((size_of(FIRST_SUM), count, rank), jnp.bfloat16),
+                exchanged(spread, SECOND_SUM),
+            )
+            pieces = from_partner(data, shift)
+            return pieces, exchanged(some, FIRST_SUM)
 
         return branch
 
-    pieces, pivot_some = lax.switch(
+    pieces, pivot_all = lax.switch(
         round_index[0] - 1, [fetch(k) for k in range(1, MAX_SHIFT + 1)], quad, pivot_part
     )
-    spread = jnp.broadcast_to(pivot_some[None], (size_of(FIRST_SUM), count, rank))
-    pivot_all = exchanged(spread, FIRST_SUM)
 
     product_scale = 8.0 / math.sqrt(block_points)
     flops = (width * row_count) ** 2 * (count + EXTRA + probe_count)
     exps = (width * row_count) ** 2 // 2
     ahead = ((lax.axis_index("x") + lax.axis_index(GROUP_AXES) + 1) % 2).astype(jnp.int32).reshape(1)
-    first, quadratic_part, row_all, col_all = local(
+    packed_sums = (probe_count + 1) * rank
+    first, spread, row_all, col_all = local(
         functools.partial(
             first_half_kernel,
             count=count,
@@ -287,28 +297,18 @@
         "first_half",
         (
             shape((width, probe_count, row_count), jnp.float32),
-            shape((probe_count, rank), jnp.float32),
+            shape((size_of(FIRST_SUM), 1, packed_sums), jnp.float32),
             shape((width, count + EXTRA, row_count), jnp.bfloat16),
             shape((width, row_count, count + EXTRA), jnp.bfloat16),
         ),
         ahead,
         quad,
         pieces,
+        pivot_all,
+        pivot_here,
         scalars=1,
         flops=flops,
         exps=exps,
-    )
-    packed_sums = (probe_count + 1) * rank
-    spread = local(
-        functools.partial(projection_kernel, count=count),
-        "projection",
-        shape((size_of(FIRST_SUM), 1, packed_sums), jnp.float32),
-        pivot_all,
-        pivot_here,
-        quad,
-        quadratic_part,
-        flops=2 * width * row_count * rank * (count + EXTRA + probe_count),
-        exps=width * row_count * rank,
     )
     some = exchanged(spread, FIRST_SUM)
     sums = local(

time: 95.3 us -> 86.7 us (0.910)
  blocking collectives: 22.1 us -> 17.6 us
  starting transfers between devices: 37.4 us -> 35.7 us
  waiting for transfers between devices: 15.4 us -> 14.3 us
    all_to_all x4, starting transfers between devices: 30.4 us -> 25.1 us  [exchanged(): return lax.all_to_all(x, axes, 0, 0)]
    all_to_all x2, blocking collectives: 22.1 us -> 17.6 us  [exchanged(): return lax.all_to_all(x, axes, 0, 0)]
    ppermute x1, starting transfers between devices: 7.04 us -> 10.6 us  [from_partner(): return lax.ppermute(x, ALL_AXES, pairs)]
    ppermute x1, waiting for transfers between devices: 2.03 us -> 0.01 us  [from_partner(): return lax.ppermute(x, ALL_AXES, pairs)]
    all_to_all x4, waiting for transfers between devices: 13.4 us -> 14.3 us  [exchanged(): return lax.all_to_all(x, axes, 0, 0)]
  transfers between devices with their start and end apart: 5 -> 5, of which waited for: 5 -> 3; matrix products, arithmetic and copies ran while one was open for 1% -> 0% of each run, Pallas kernels for 12% -> 7%
where the time goes in v5:
time: 86.7 us; the launch traced here: 86.1 us
  starting transfers between devices  35.7 us (41%)
  blocking collectives  17.6 us (20%)
  Pallas kernels  15.8 us (18%)
  waiting for transfers between devices  14.3 us (16%)
  between operations  1.36 us (2%)
  local copies, waits for them, and re-layouts  1.27 us (1%)
    all_to_all x4, starting transfers between devices, exchanged(): return lax.all_to_all(x, axes, 0, 0)  25.1 us
    all_to_all x2, blocking collectives, exchanged(): return lax.all_to_all(x, axes, 0, 0)  17.6 us
    pallas_call x8, Pallas kernels, local(): pl.pallas_call(kernel, name=name, out_shape=out_shape, in_specs=specs, ou...  15.8 us
    all_to_all x4, waiting for transfers between devices, exchanged(): return lax.all_to_all(x, axes, 0, 0)  14.3 us
    ppermute x1, starting transfers between devices, from_partner(): return lax.ppermute(x, ALL_AXES, pairs)  10.6 us
  transfers between devices with their start and end apart: 5, of which 3 were waited for; matrix products, arithmetic and copies ran while one was open for 0% of the time, Pallas kernels for 7%

profile of v5, /device:TPU:1, one launch (start us, length us, event | category | flops | bytes accessed | tf_op | source)
XLA Modules:
  0.0 86.1 jit_solution(14399614829563512247)
XLA Ops:
  0.6 1.7 %prepare.1.packed_ref = bf16[4,40,768]{2,1,0:T(8,128)(2,1)} custom-call(f32[32,768]{1,0:T(8,128)} %feat_hbm.1, f32[1,32]{1,0:T(1,128)} %bitcast.8, bf16[8,768]{1,0:T(8,128)(2,1)} %probe_hbm.1), custom_call_target="tpu_custom_call" | custom-call | bytes 110720 | tf_op jit(solution)/shard_map/prepare/pallas_call | solution.py:48
  2.4 0.0 copy-start
  2.4 5.0 %all-to-all-start.62 = ((bf16[4,40,768]{2,1,0:T(8,128)(2,1)}), bf16[4,40,768]{2,1,0:T(8,128)(2,1)S(1)}, u32[]{:S(2)}, u32[]{:S(2)}) async-start(bf16[4,40,768]{2,1,0:T(8,128)(2,1)} %prepare.1.packed_ref), calls=%async_computation.62 | async-start | bytes 491520 | tf_op jit(solution)/shard_map/all_to_all | solution.py:26
  8.0 0.0 copy-start.1
  8.0 0.0 copy-done
  8.0 0.6 copy-done.1
  8.7 0.2 own_pivots.1
  8.9 3.9 %all-to-all-done.62.row_ref = bf16[4,40,768]{2,1,0:T(8,128)(2,1)S(1)} async-done(((bf16[4,40,768]{2,1,0:T(8,128)(2,1)}), bf16[4,40,768]{2,1,0:T(8,128)(2,1)S(1)}, u32[]{:S(2)}, u32[]{:S(2)}) %all-to-all-start.62) | async-done | bytes 245792 | tf_op jit(solution)/shard_map/all_to_all | solution.py:26
  12.8 38.0 %conditional.1 = (bf16[4,40,768]{2,1,0:T(8,128)(2,1)}, bf16[16,32,128]{2,1,0:T(8,128)(2,1)}) conditional(s32[]{:T(128)} %bitcast.2, (bf16[4,40,768]{2,1,0:T(8,128)(2,1)S(1)}, bf16[32,128]{1,0:T(8,128)(2,1)S(1)}) %tuple.131, (bf16[4,40,768]{2,1,0:T(8,128)(2,1)S(1)}, bf16[32,128]{1,0:T(8,128)(2,1)S(1)}) %tuple.131, ...), branch_computations={%region_0.1_spmd, %region_1.2_spmd, %region_2.3_spmd, %region_3.4_... | conditional | bytes 1712248 | solution.py:282
  12.8 0.6 broadcast_in_dim.65
  13.4 10.1 %all-to-all-start.4 = ((bf16[8,32,128]{2,1,0:T(8,128)(2,1)}), bf16[8,32,128]{2,1,0:T(8,128)(2,1)S(1)}, u32[]{:S(2)}, u32[]{:S(2)}) async-start(bf16[8,32,128]{2,1,0:T(8,128)(2,1)} %broadcast_in_dim.65), calls=%async_computation.4 | async-start | bytes 131072 | tf_op jit(solution)/shard_map/cond/branch_2_fun/all_to_all | solution.py:26
  23.5 10.6 %collective-permute-start.2 = (bf16[4,40,768]{2,1,0:T(8,128)(2,1)S(1)}, bf16[4,40,768]{2,1,0:T(8,128)(2,1)}, u32[]{:S(2)}, u32[]{:S(2)}) collective-permute-start(bf16[4,40,768]{2,1,0:T(8,128)(2,1)S(1)} %get-tuple-element.128), channel_id=1, source_target_pairs={{24,0},{489,1},{30,2},{495,3},{28,4},{493,5},{26,6},{491,7},{496,8... | collective-permute-start | bytes 737288 | tf_op jit(solution)/shard_map/cond/branch_2_fun/ppermute | solution.py:39
  34.1 0.0 all-to-all-done.4.in_ref
  34.1 0.7 pivot_sum.33
  34.8 6.7 %all-to-all-start.5 = ((bf16[16,32,128]{2,1,0:T(8,128)(2,1)}), bf16[16,32,128]{2,1,0:T(8,128)(2,1)}, u32[]{:S(2)}, u32[]{:S(2)}) async-start(bf16[16,32,128]{2,1,0:T(8,128)(2,1)} %pivot_sum.33), calls=%async_computation.5 | async-start | bytes 262144 | tf_op jit(solution)/shard_map/cond/branch_2_fun/all_to_all | solution.py:26
  41.5 0.0 collective-permute-done.2
  41.5 9.3 %all-to-all-done.5 = bf16[16,32,128]{2,1,0:T(8,128)(2,1)} async-done(((bf16[16,32,128]{2,1,0:T(8,128)(2,1)}), bf16[16,32,128]{2,1,0:T(8,128)(2,1)}, u32[]{:S(2)}, u32[]{:S(2)}) %all-to-all-start.5) | async-done | bytes 131104 | tf_op jit(solution)/shard_map/cond/branch_2_fun/all_to_all | solution.py:26
  50.8 6.6 %first_half.1 = (f32[4,8,768]{2,1,0:T(8,128)S(1)}, f32[16,1,1152]{2,1,0:T(1,128)S(1)}, bf16[4,48,768]{2,1,0:T(8,128)(2,1)S(1)}, bf16[4,768,48]{2,1,0:T(8,128)(2,1)S(1)}) custom-call(s32[1]{0:T(128)} %bitcast.ahead_ref, bf16[4,40,768]{2,1,0:T(8,128)(2,1)S(1)} %all-to-all-done.62.row_ref, bf16[4,40,768]{2,1,0:T(8,128)(2,1)} %get-tuple-element.195.col_ref, ...), custom_call_target="tpu_custom_call" | custom-call | flops 528482304 | bytes 623108 | tf_op jit(solution)/shard_map/first_half/pallas_call | solution.py:48
  57.4 10.4 %all_to_all.268.in_ref = f32[16,1,1152]{2,1,0:T(1,128)S(1)} all-to-all(f32[16,1,1152]{2,1,0:T(1,128)S(1)} %get-tuple-element.200), channel_id=1, replica_groups=mesh['y'=8,'zlo'=4,'core'=2,'zhi'=2,'x'=4] {'y','core'}, dimensions={0} | all-to-all | bytes 147456 | tf_op jit(solution)/shard_map/all_to_all | solution.py:26
  67.8 0.6 first_sum.1
  68.4 3.3 %all-to-all-start.64 = ((f32[8,1,1152]{2,1,0:T(1,128)}), f32[8,1,1152]{2,1,0:T(1,128)S(1)}, u32[]{:S(2)}, u32[]{:S(2)}) async-start(f32[8,1,1152]{2,1,0:T(1,128)} %first_sum.1), calls=%async_computation.64 | async-start | bytes 73728 | tf_op jit(solution)/shard_map/all_to_all | solution.py:26
  71.8 5.4 %second_half.1.sum_ref = f32[4,8,768]{2,1,0:T(8,128)S(1)} custom-call(s32[1]{0:T(128)} %bitcast.ahead_ref, bf16[4,48,768]{2,1,0:T(8,128)(2,1)S(1)} %get-tuple-element.197.row_all, bf16[4,768,48]{2,1,0:T(8,128)(2,1)S(1)} %get-tuple-element.198.col_all, bf16[4,40,768]{2,1,0:T(8,128)(2,1)} %get-tuple-element.195.col_ref, ...), custom_call_target="tpu_custom_call" | custom-call | flops 528482304 | bytes 933892 | tf_op jit(solution)/shard_map/second_half/pallas_call | solution.py:48
  77.2 1.1 %all-to-all-done.64.total_ref = f32[8,1,1152]{2,1,0:T(1,128)S(1)} async-done(((f32[8,1,1152]{2,1,0:T(1,128)}), f32[8,1,1152]{2,1,0:T(1,128)S(1)}, u32[]{:S(2)}, u32[]{:S(2)}) %all-to-all-start.64) | async-done | bytes 36896 | tf_op jit(solution)/shard_map/all_to_all | solution.py:26
  78.3 7.2 %all_to_all.269.in_ref = f32[4,8,1024]{2,1,0:T(8,128)S(1)} all-to-all(f32[4,8,1024]{2,1,0:T(8,128)S(1)} %join.1), channel_id=1, replica_groups=mesh['y'=8,'zlo'=4,'core'=2,'zhi'=2,'x'=4] {'x'}, dimensions={0} | all-to-all | bytes 262144 | tf_op jit(solution)/shard_map/all_to_all | solution.py:26
  85.5 0.6 finish.1
  (2 shorter events, 0.0 us)
Async XLA Ops:
  2.4 5.7 %copy-start = (bf16[4,40,768]{2,1,0:T(8,128)(2,1)S(1)}, bf16[4,40,768]{2,1,0:T(8,128)(2,1)}, u32[]{:S(2)}) copy-start(bf16[4,40,768]{2,1,0:T(8,128)(2,1)} %prepare.1.packed_ref) | copy-start | bytes 737284
  2.4 10.4 %all-to-all-start.62 = ((bf16[4,40,768]{2,1,0:T(8,128)(2,1)}), bf16[4,40,768]{2,1,0:T(8,128)(2,1)S(1)}, u32[]{:S(2)}, u32[]{:S(2)}) async-start(bf16[4,40,768]{2,1,0:T(8,128)(2,1)} %prepare.1.packed_ref), calls=%async_computation.62 | async-start | bytes 491520 | tf_op jit(solution)/shard_map/all_to_all | solution.py:26
  8.0 0.7 copy-start.1
  13.4 20.7 %all-to-all-start.4 = ((bf16[8,32,128]{2,1,0:T(8,128)(2,1)}), bf16[8,32,128]{2,1,0:T(8,128)(2,1)S(1)}, u32[]{:S(2)}, u32[]{:S(2)}) async-start(bf16[8,32,128]{2,1,0:T(8,128)(2,1)} %broadcast_in_dim.65), calls=%async_computation.4 | async-start | bytes 131072 | tf_op jit(solution)/shard_map/cond/branch_2_fun/all_to_all | solution.py:26
  23.5 18.0 %collective-permute-start.2 = (bf16[4,40,768]{2,1,0:T(8,128)(2,1)S(1)}, bf16[4,40,768]{2,1,0:T(8,128)(2,1)}, u32[]{:S(2)}, u32[]{:S(2)}) collective-permute-start(bf16[4,40,768]{2,1,0:T(8,128)(2,1)S(1)} %get-tuple-element.128), channel_id=1, source_target_pairs={{24,0},{489,1},{30,2},{495,3},{28,4},{493,5},{26,6},{491,7},{496,8... | collective-permute-start | bytes 737288 | tf_op jit(solution)/shard_map/cond/branch_2_fun/ppermute | solution.py:39
  34.8 16.0 %all-to-all-start.5 = ((bf16[16,32,128]{2,1,0:T(8,128)(2,1)}), bf16[16,32,128]{2,1,0:T(8,128)(2,1)}, u32[]{:S(2)}, u32[]{:S(2)}) async-start(bf16[16,32,128]{2,1,0:T(8,128)(2,1)} %pivot_sum.33), calls=%async_computation.5 | async-start | bytes 262144 | tf_op jit(solution)/shard_map/cond/branch_2_fun/all_to_all | solution.py:26
  68.4 9.9 %all-to-all-start.64 = ((f32[8,1,1152]{2,1,0:T(1,128)}), f32[8,1,1152]{2,1,0:T(1,128)S(1)}, u32[]{:S(2)}, u32[]{:S(2)}) async-start(f32[8,1,1152]{2,1,0:T(1,128)} %first_sum.1), calls=%async_computation.64 | async-start | bytes 73728 | tf_op jit(solution)/shard_map/all_to_all | solution.py:26

commit v6 on v5

--- a/solution.py
+++ b/solution.py
@@ -98,12 +98,13 @@
 
 
 def own_pivots_kernel(first_ref, packed_ref, pivot_ref, out_ref):
-    count, rank = out_ref.shape
+    count, rank = out_ref.shape[1:]
     points = packed_ref.shape[2]
     point = lax.broadcasted_iota(jnp.int32, (points, rank), 0) + first_ref[0]
     mask = jnp.where(point == pivot_ref[...], 1.0, 0.0).astype(jnp.bfloat16)
     part = jnp.dot(packed_ref[0, :count], mask, preferred_element_type=jnp.float32)
-    out_ref[...] = part.astype(jnp.bfloat16)
+    for copy in range(out_ref.shape[0]):
+        out_ref[copy] = part.astype(jnp.bfloat16)
 
 
 def sum_spread_kernel(in_ref, out_ref):
@@ -256,7 +257,7 @@
     pivot_part = local(
         own_pivots_kernel,
         "own_pivots",
-        shape((count, rank), jnp.bfloat16),
+        shape((size_of(SECOND_SUM), count, rank), jnp.bfloat16),
         first_point.reshape(1),
         packed,
         pivot_row,
@@ -267,12 +268,11 @@
 
     def fetch(shift):
         def branch(data, part):
-            spread = jnp.broadcast_to(part[None], (size_of(SECOND_SUM),) + part.shape)
             some = local(
                 sum_spread_kernel,
                 "pivot_sum",
                 shape((size_of(FIRST_SUM), count, rank), jnp.bfloat16),
-                exchanged(spread, SECOND_SUM),
+                exchanged(part, SECOND_SUM),
             )
             pieces = from_partner(data, shift)
             return pieces, exchanged(some, FIRST_SUM)

time: 86.7 us -> 93.7 us (1.081)
  starting transfers between devices: 35.7 us -> 40.9 us
  waiting for transfers between devices: 14.3 us -> 16 us
    all_to_all x4, starting transfers between devices: 25.1 us -> 36.7 us  [exchanged(): return lax.all_to_all(x, axes, 0, 0)]
    ppermute x1, starting transfers between devices: 10.6 us -> 4.26 us  [from_partner(): return lax.ppermute(x, ALL_AXES, pairs)]
    all_to_all x4, waiting for transfers between devices: 14.3 us -> 16 us  [exchanged(): return lax.all_to_all(x, axes, 0, 0)]
  transfers between devices with their start and end apart: 5 -> 5, of which waited for: 3 -> 4; matrix products, arithmetic and copies ran while one was open for 0% -> 0% of each run, Pallas kernels for 7% -> 7%
where the time goes in v6:
time: 93.7 us; the launch traced here: 93.1 us
  starting transfers between devices  40.9 us (44%)
  blocking collectives  17.6 us (19%)
  Pallas kernels  16.5 us (18%)
  waiting for transfers between devices  16 us (17%)
  between operations  1.35 us (1%)
    all_to_all x4, starting transfers between devices, exchanged(): return lax.all_to_all(x, axes, 0, 0)  36.7 us
    all_to_all x2, blocking collectives, exchanged(): return lax.all_to_all(x, axes, 0, 0)  17.6 us
    pallas_call x8, Pallas kernels, local(): pl.pallas_call(kernel, name=name, out_shape=out_shape, in_specs=specs, ou...  16.5 us
    all_to_all x4, waiting for transfers between devices, exchanged(): return lax.all_to_all(x, axes, 0, 0)  16 us
    ppermute x1, starting transfers between devices, from_partner(): return lax.ppermute(x, ALL_AXES, pairs)  4.26 us
  transfers between devices with their start and end apart: 5, of which 4 were waited for; matrix products, arithmetic and copies ran while one was open for 0% of the time, Pallas kernels for 7%

profile of v6, /device:TPU:1, one launch (start us, length us, event | category | flops | bytes accessed | tf_op | source)
XLA Modules:
  0.0 93.1 jit_solution(8522373269927314070)
XLA Ops:
  0.6 1.7 %prepare.1.packed_ref = bf16[4,40,768]{2,1,0:T(8,128)(2,1)} custom-call(f32[32,768]{1,0:T(8,128)} %feat_hbm.1, f32[1,32]{1,0:T(1,128)} %bitcast.8, bf16[8,768]{1,0:T(8,128)(2,1)} %probe_hbm.1), custom_call_target="tpu_custom_call" | custom-call | bytes 110720 | tf_op jit(solution)/shard_map/prepare/pallas_call | solution.py:48
  2.4 0.0 copy-start
  2.4 5.0 %all-to-all-start.62 = ((bf16[4,40,768]{2,1,0:T(8,128)(2,1)}), bf16[4,40,768]{2,1,0:T(8,128)(2,1)S(1)}, u32[]{:S(2)}, u32[]{:S(2)}) async-start(bf16[4,40,768]{2,1,0:T(8,128)(2,1)} %prepare.1.packed_ref), calls=%async_computation.62 | async-start | bytes 491520 | tf_op jit(solution)/shard_map/all_to_all | solution.py:26
  8.0 0.0 copy-start.1
  8.0 0.0 copy-done
  8.0 0.6 copy-done.1
  8.7 0.8 own_pivots.1
  9.5 3.3 %all-to-all-done.62.row_ref = bf16[4,40,768]{2,1,0:T(8,128)(2,1)S(1)} async-done(((bf16[4,40,768]{2,1,0:T(8,128)(2,1)}), bf16[4,40,768]{2,1,0:T(8,128)(2,1)S(1)}, u32[]{:S(2)}, u32[]{:S(2)}) %all-to-all-start.62) | async-done | bytes 245792 | tf_op jit(solution)/shard_map/all_to_all | solution.py:26
  12.8 44.9 %conditional.1 = (bf16[4,40,768]{2,1,0:T(8,128)(2,1)}, bf16[16,32,128]{2,1,0:T(8,128)(2,1)}) conditional(s32[]{:T(128)} %bitcast.2, (bf16[4,40,768]{2,1,0:T(8,128)(2,1)S(1)}, bf16[8,32,128]{2,1,0:T(8,128)(2,1)}) %tuple.131, (bf16[4,40,768]{2,1,0:T(8,128)(2,1)S(1)}, bf16[8,32,128]{2,1,0:T(8,128)(2,1)}) %tuple.131, ...), branch_computations={%region_0.1_spmd, %region_1.2_spmd, %region_2.3_spmd, %region_3.4_... | conditional | bytes 1638520 | solution.py:282
  12.8 10.1 %all-to-all-start.6 = ((bf16[8,32,128]{2,1,0:T(8,128)(2,1)}), bf16[8,32,128]{2,1,0:T(8,128)(2,1)S(1)}, u32[]{:S(2)}, u32[]{:S(2)}) async-start(bf16[8,32,128]{2,1,0:T(8,128)(2,1)} %get-tuple-element.131), calls=%async_computation.6 | async-start | bytes 131072 | tf_op jit(solution)/shard_map/cond/branch_3_fun/all_to_all | solution.py:26
  22.9 4.3 %collective-permute-start.3 = (bf16[4,40,768]{2,1,0:T(8,128)(2,1)S(1)}, bf16[4,40,768]{2,1,0:T(8,128)(2,1)}, u32[]{:S(2)}, u32[]{:S(2)}) collective-permute-start(bf16[4,40,768]{2,1,0:T(8,128)(2,1)S(1)} %get-tuple-element.130), channel_id=1, source_target_pairs={{32,0},{481,1},{38,2},{487,3},{36,4},{485,5},{34,6},{483,7},{488,8... | collective-permute-start | bytes 737288 | tf_op jit(solution)/shard_map/cond/branch_3_fun/ppermute | solution.py:39
  27.1 2.4 %all-to-all-done.6.in_ref = bf16[8,32,128]{2,1,0:T(8,128)(2,1)S(1)} async-done(((bf16[8,32,128]{2,1,0:T(8,128)(2,1)}), bf16[8,32,128]{2,1,0:T(8,128)(2,1)S(1)}, u32[]{:S(2)}, u32[]{:S(2)}) %all-to-all-start.6) | async-done | bytes 65568 | tf_op jit(solution)/shard_map/cond/branch_3_fun/all_to_all | solution.py:26
  29.5 0.7 pivot_sum.34
  30.2 18.3 %all-to-all-start.7 = ((bf16[16,32,128]{2,1,0:T(8,128)(2,1)}), bf16[16,32,128]{2,1,0:T(8,128)(2,1)}, u32[]{:S(2)}, u32[]{:S(2)}) async-start(bf16[16,32,128]{2,1,0:T(8,128)(2,1)} %pivot_sum.34), calls=%async_computation.7 | async-start | bytes 262144 | tf_op jit(solution)/shard_map/cond/branch_3_fun/all_to_all | solution.py:26
  48.5 0.0 collective-permute-done.3
  48.5 9.3 %all-to-all-done.7 = bf16[16,32,128]{2,1,0:T(8,128)(2,1)} async-done(((bf16[16,32,128]{2,1,0:T(8,128)(2,1)}), bf16[16,32,128]{2,1,0:T(8,128)(2,1)}, u32[]{:S(2)}, u32[]{:S(2)}) %all-to-all-start.7) | async-done | bytes 131104 | tf_op jit(solution)/shard_map/cond/branch_3_fun/all_to_all | solution.py:26
  57.7 6.6 %first_half.1 = (f32[4,8,768]{2,1,0:T(8,128)S(1)}, f32[16,1,1152]{2,1,0:T(1,128)S(1)}, bf16[4,48,768]{2,1,0:T(8,128)(2,1)S(1)}, bf16[4,768,48]{2,1,0:T(8,128)(2,1)S(1)}) custom-call(s32[1]{0:T(128)} %bitcast.ahead_ref, bf16[4,40,768]{2,1,0:T(8,128)(2,1)S(1)} %all-to-all-done.62.row_ref, bf16[4,40,768]{2,1,0:T(8,128)(2,1)} %get-tuple-element.195.col_ref, ...), custom_call_target="tpu_custom_call" | custom-call | flops 528482304 | bytes 623108 | tf_op jit(solution)/shard_map/first_half/pallas_call | solution.py:48
  64.3 10.4 %all_to_all.268.in_ref = f32[16,1,1152]{2,1,0:T(1,128)S(1)} all-to-all(f32[16,1,1152]{2,1,0:T(1,128)S(1)} %get-tuple-element.200), channel_id=1, replica_groups=mesh['y'=8,'zlo'=4,'core'=2,'zhi'=2,'x'=4] {'y','core'}, dimensions={0} | all-to-all | bytes 147456 | tf_op jit(solution)/shard_map/all_to_all | solution.py:26
  74.7 0.6 first_sum.1
  75.4 3.3 %all-to-all-start.64 = ((f32[8,1,1152]{2,1,0:T(1,128)}), f32[8,1,1152]{2,1,0:T(1,128)S(1)}, u32[]{:S(2)}, u32[]{:S(2)}) async-start(f32[8,1,1152]{2,1,0:T(1,128)} %first_sum.1), calls=%async_computation.64 | async-start | bytes 73728 | tf_op jit(solution)/shard_map/all_to_all | solution.py:26
  78.7 5.4 %second_half.1.sum_ref = f32[4,8,768]{2,1,0:T(8,128)S(1)} custom-call(s32[1]{0:T(128)} %bitcast.ahead_ref, bf16[4,48,768]{2,1,0:T(8,128)(2,1)S(1)} %get-tuple-element.197.row_all, bf16[4,768,48]{2,1,0:T(8,128)(2,1)S(1)} %get-tuple-element.198.col_all, bf16[4,40,768]{2,1,0:T(8,128)(2,1)} %get-tuple-element.195.col_ref, ...), custom_call_target="tpu_custom_call" | custom-call | flops 528482304 | bytes 933892 | tf_op jit(solution)/shard_map/second_half/pallas_call | solution.py:48
  84.1 1.1 %all-to-all-done.64.total_ref = f32[8,1,1152]{2,1,0:T(1,128)S(1)} async-done(((f32[8,1,1152]{2,1,0:T(1,128)}), f32[8,1,1152]{2,1,0:T(1,128)S(1)}, u32[]{:S(2)}, u32[]{:S(2)}) %all-to-all-start.64) | async-done | bytes 36896 | tf_op jit(solution)/shard_map/all_to_all | solution.py:26
  85.2 7.2 %all_to_all.269.in_ref = f32[4,8,1024]{2,1,0:T(8,128)S(1)} all-to-all(f32[4,8,1024]{2,1,0:T(8,128)S(1)} %join.1), channel_id=1, replica_groups=mesh['y'=8,'zlo'=4,'core'=2,'zhi'=2,'x'=4] {'x'}, dimensions={0} | all-to-all | bytes 262144 | tf_op jit(solution)/shard_map/all_to_all | solution.py:26
  92.5 0.6 finish.1
  (2 shorter events, 0.0 us)
Async XLA Ops:
  2.4 5.7 %copy-start = (bf16[4,40,768]{2,1,0:T(8,128)(2,1)S(1)}, bf16[4,40,768]{2,1,0:T(8,128)(2,1)}, u32[]{:S(2)}) copy-start(bf16[4,40,768]{2,1,0:T(8,128)(2,1)} %prepare.1.packed_ref) | copy-start | bytes 737284
  2.4 10.4 %all-to-all-start.62 = ((bf16[4,40,768]{2,1,0:T(8,128)(2,1)}), bf16[4,40,768]{2,1,0:T(8,128)(2,1)S(1)}, u32[]{:S(2)}, u32[]{:S(2)}) async-start(bf16[4,40,768]{2,1,0:T(8,128)(2,1)} %prepare.1.packed_ref), calls=%async_computation.62 | async-start | bytes 491520 | tf_op jit(solution)/shard_map/all_to_all | solution.py:26
  8.0 0.7 copy-start.1
  12.8 16.7 %all-to-all-start.6 = ((bf16[8,32,128]{2,1,0:T(8,128)(2,1)}), bf16[8,32,128]{2,1,0:T(8,128)(2,1)S(1)}, u32[]{:S(2)}, u32[]{:S(2)}) async-start(bf16[8,32,128]{2,1,0:T(8,128)(2,1)} %get-tuple-element.131), calls=%async_computation.6 | async-start | bytes 131072 | tf_op jit(solution)/shard_map/cond/branch_3_fun/all_to_all | solution.py:26
  22.9 25.6 %collective-permute-start.3 = (bf16[4,40,768]{2,1,0:T(8,128)(2,1)S(1)}, bf16[4,40,768]{2,1,0:T(8,128)(2,1)}, u32[]{:S(2)}, u32[]{:S(2)}) collective-permute-start(bf16[4,40,768]{2,1,0:T(8,128)(2,1)S(1)} %get-tuple-element.130), channel_id=1, source_target_pairs={{32,0},{481,1},{38,2},{487,3},{36,4},{485,5},{34,6},{483,7},{488,8... | collective-permute-start | bytes 737288 | tf_op jit(solution)/shard_map/cond/branch_3_fun/ppermute | solution.py:39
  30.2 27.6 %all-to-all-start.7 = ((bf16[16,32,128]{2,1,0:T(8,128)(2,1)}), bf16[16,32,128]{2,1,0:T(8,128)(2,1)}, u32[]{:S(2)}, u32[]{:S(2)}) async-start(bf16[16,32,128]{2,1,0:T(8,128)(2,1)} %pivot_sum.34), calls=%async_computation.7 | async-start | bytes 262144 | tf_op jit(solution)/shard_map/cond/branch_3_fun/all_to_all | solution.py:26
  75.4 9.9 %all-to-all-start.64 = ((f32[8,1,1152]{2,1,0:T(1,128)}), f32[8,1,1152]{2,1,0:T(1,128)S(1)}, u32[]{:S(2)}, u32[]{:S(2)}) async-start(f32[8,1,1152]{2,1,0:T(1,128)} %first_sum.1), calls=%async_computation.64 | async-start | bytes 73728 | tf_op jit(solution)/shard_map/all_to_all | solution.py:26

commit v7 on v6

--- a/solution.py
+++ b/solution.py
@@ -115,11 +115,10 @@
         out_ref[copy] = total.astype(out_ref.dtype)
 
 
-def pair_sum(row_all, col_all, col_ref, place, other, count, probes):
+def pair_sum(row_all, col_all, col_probe, place, other):
     power = jnp.dot(col_all[other], row_all[place], preferred_element_type=jnp.float32)
     kernel = jnp.exp(power).astype(jnp.bfloat16)
-    col_probe = col_ref[other, count : count + probes]
-    return jnp.dot(col_probe, kernel, preferred_element_type=jnp.float32)
+    return jnp.dot(col_probe[other], kernel, preferred_element_type=jnp.float32)
 
 
 def first_half_kernel(
@@ -132,6 +131,7 @@
     out_ref,
     row_all,
     col_all,
+    col_probe,
     *,
     count,
     scale,
@@ -141,16 +141,20 @@
     for place in range(width):
         row_all[place] = extended(row_ref[place, :count], True)
         col_all[place] = turned(extended(col_ref[place, :count], False))
+        col_probe[place] = col_ref[place, count : count + probes]
     sum_ref[...] = jnp.zeros_like(sum_ref)
 
     def step(turn, carry):
-        for part in range(4):
-            place = jnp.where(ahead, 2 * turn + part // 2, 2 + turn)
-            other = jnp.where(ahead, part % 2, part)
-            sum_ref[place] += pair_sum(row_all, col_all, col_ref, place, other, count, probes)
+        for part in range(2):
+            place = jnp.where(ahead, 2 * turn + part, 2 + turn)
+            first = jnp.where(ahead, 0, 2 * part)
+            sum_ref[place] += pair_sum(row_all, col_all, col_probe, place, first) + pair_sum(
+                row_all, col_all, col_probe, place, first + 1
+            )
         return carry
 
-    lax.fori_loop(0, 2, step, 0)
+    for turn in range(2):
+        step(turn, 0)
     quad = jnp.zeros((probes, 1), jnp.float32)
     for place in range(width):
         row_probe = row_ref[place, count : count + probes].astype(jnp.float32)
@@ -181,10 +185,8 @@
         out_ref[copy] = packed
 
 
-def second_half_kernel(
-    ahead_ref, row_all, col_all, col_ref, first_ref, sum_ref, *, count, scale
-):
-    width, probes = first_ref.shape[:2]
+def second_half_kernel(ahead_ref, row_all, col_all, col_probe, first_ref, sum_ref, *, scale):
+    width = first_ref.shape[0]
     ahead = ahead_ref[0] == 1
     sum_ref[...] = first_ref[...]
 
@@ -192,7 +194,7 @@
         for part in range(4):
             place = jnp.where(ahead, 2 * turn + part // 2, turn)
             other = jnp.where(ahead, 2 + part % 2, part)
-            sum_ref[place] += pair_sum(row_all, col_all, col_ref, place, other, count, probes)
+            sum_ref[place] += pair_sum(row_all, col_all, col_probe, place, other)
         return carry
 
     lax.fori_loop(0, 2, step, 0)
@@ -288,7 +290,7 @@
     exps = (width * row_count) ** 2 // 2
     ahead = ((lax.axis_index("x") + lax.axis_index(GROUP_AXES) + 1) % 2).astype(jnp.int32).reshape(1)
     packed_sums = (probe_count + 1) * rank
-    first, spread, row_all, col_all = local(
+    first, spread, row_all, col_all, col_probe = local(
         functools.partial(
             first_half_kernel,
             count=count,
@@ -300,6 +302,7 @@
             shape((size_of(FIRST_SUM), 1, packed_sums), jnp.float32),
             shape((width, count + EXTRA, row_count), jnp.bfloat16),
             shape((width, row_count, count + EXTRA), jnp.bfloat16),
+            shape((width, probe_count, row_count), jnp.bfloat16),
         ),
         ahead,
         quad,
@@ -312,13 +315,13 @@
     )
     some = exchanged(spread, FIRST_SUM)
     sums = local(
-        functools.partial(second_half_kernel, count=count, scale=product_scale),
+        functools.partial(second_half_kernel, scale=product_scale),
         "second_half",
         shape((width, probe_count, row_count), jnp.float32),
         ahead,
         row_all,
         col_all,
-        pieces,
+        col_probe,
         first,
         scalars=1,
         flops=flops,

time: 93.7 us -> 92 us (0.982)
  starting transfers between devices: 40.9 us -> 32.9 us
  blocking collectives: 17.6 us -> 23.4 us
  waiting for transfers between devices: 16 us -> 18 us
  Pallas kernels: 16.5 us -> 14.6 us
    all_to_all x4, starting transfers between devices: 36.7 us -> 29.6 us  [exchanged(): return lax.all_to_all(x, axes, 0, 0)]
    all_to_all x2, blocking collectives: 17.6 us -> 23.4 us  [exchanged(): return lax.all_to_all(x, axes, 0, 0)]
    all_to_all x4, waiting for transfers between devices: 16 us -> 18 us  [exchanged(): return lax.all_to_all(x, axes, 0, 0)]
    pallas_call x8, Pallas kernels: 16.5 us -> 14.6 us  [local(): pl.pallas_call(kernel, name=name, out_shape=out_shape, in_specs=specs, ou...]
where the time goes in v7:
time: 92 us; the launch traced here: 91 us
  starting transfers between devices  32.9 us (36%)
  blocking collectives  23.4 us (25%)
  waiting for transfers between devices  18 us (20%)
  Pallas kernels  14.6 us (16%)
  between operations  1.35 us (1%)
    all_to_all x4, starting transfers between devices, exchanged(): return lax.all_to_all(x, axes, 0, 0)  29.6 us
    all_to_all x2, blocking collectives, exchanged(): return lax.all_to_all(x, axes, 0, 0)  23.4 us
    all_to_all x4, waiting for transfers between devices, exchanged(): return lax.all_to_all(x, axes, 0, 0)  18 us
    pallas_call x8, Pallas kernels, local(): pl.pallas_call(kernel, name=name, out_shape=out_shape, in_specs=specs, ou...  14.6 us
    ppermute x1, starting transfers between devices, from_partner(): return lax.ppermute(x, ALL_AXES, pairs)  3.36 us
  transfers between devices with their start and end apart: 5, of which 4 were waited for; matrix products, arithmetic and copies ran while one was open for 0% of the time, Pallas kernels for 7%

profile of v7, /device:TPU:1, one launch (start us, length us, event | category | flops | bytes accessed | tf_op | source)
XLA Modules:
  0.0 91.0 jit_solution(8962106613325420423)
XLA Ops:
  0.6 1.7 %prepare.1.packed_ref = bf16[4,40,768]{2,1,0:T(8,128)(2,1)} custom-call(f32[32,768]{1,0:T(8,128)} %feat_hbm.1, f32[1,32]{1,0:T(1,128)} %bitcast.8, bf16[8,768]{1,0:T(8,128)(2,1)} %probe_hbm.1), custom_call_target="tpu_custom_call" | custom-call | bytes 110720 | tf_op jit(solution)/shard_map/prepare/pallas_call | solution.py:48
  2.4 0.0 copy-start
  2.4 5.0 %all-to-all-start.62 = ((bf16[4,40,768]{2,1,0:T(8,128)(2,1)}), bf16[4,40,768]{2,1,0:T(8,128)(2,1)S(1)}, u32[]{:S(2)}, u32[]{:S(2)}) async-start(bf16[4,40,768]{2,1,0:T(8,128)(2,1)} %prepare.1.packed_ref), calls=%async_computation.62 | async-start | bytes 491520 | tf_op jit(solution)/shard_map/all_to_all | solution.py:26
  8.0 0.0 copy-start.1
  8.0 0.0 copy-done
  8.0 0.6 copy-done.1
  8.7 0.8 own_pivots.1
  9.5 3.3 %all-to-all-done.62.row_ref = bf16[4,40,768]{2,1,0:T(8,128)(2,1)S(1)} async-done(((bf16[4,40,768]{2,1,0:T(8,128)(2,1)}), bf16[4,40,768]{2,1,0:T(8,128)(2,1)S(1)}, u32[]{:S(2)}, u32[]{:S(2)}) %all-to-all-start.62) | async-done | bytes 245792 | tf_op jit(solution)/shard_map/all_to_all | solution.py:26
  12.8 37.4 %conditional.1 = (bf16[4,40,768]{2,1,0:T(8,128)(2,1)}, bf16[16,32,128]{2,1,0:T(8,128)(2,1)}) conditional(s32[]{:T(128)} %bitcast.2, (bf16[4,40,768]{2,1,0:T(8,128)(2,1)S(1)}, bf16[8,32,128]{2,1,0:T(8,128)(2,1)}) %tuple.131, (bf16[4,40,768]{2,1,0:T(8,128)(2,1)S(1)}, bf16[8,32,128]{2,1,0:T(8,128)(2,1)}) %tuple.131, ...), branch_computations={%region_0.1_spmd, %region_1.2_spmd, %region_2.3_spmd, %region_3.4_... | conditional | bytes 1638520 | solution.py:284
  12.8 10.1 %all-to-all-start.2 = ((bf16[8,32,128]{2,1,0:T(8,128)(2,1)}), bf16[8,32,128]{2,1,0:T(8,128)(2,1)S(1)}, u32[]{:S(2)}, u32[]{:S(2)}) async-start(bf16[8,32,128]{2,1,0:T(8,128)(2,1)} %get-tuple-element.127), calls=%async_computation.2 | async-start | bytes 131072 | tf_op jit(solution)/shard_map/cond/branch_1_fun/all_to_all | solution.py:26
  22.9 3.4 %collective-permute-start.1 = (bf16[4,40,768]{2,1,0:T(8,128)(2,1)S(1)}, bf16[4,40,768]{2,1,0:T(8,128)(2,1)}, u32[]{:S(2)}, u32[]{:S(2)}) collective-permute-start(bf16[4,40,768]{2,1,0:T(8,128)(2,1)S(1)} %get-tuple-element.126), channel_id=1, source_target_pairs={{16,0},{497,1},{22,2},{503,3},{20,4},{501,5},{18,6},{499,7},{504,8... | collective-permute-start | bytes 737288 | tf_op jit(solution)/shard_map/cond/branch_1_fun/ppermute | solution.py:39
  26.2 3.3 %all-to-all-done.2.in_ref = bf16[8,32,128]{2,1,0:T(8,128)(2,1)S(1)} async-done(((bf16[8,32,128]{2,1,0:T(8,128)(2,1)}), bf16[8,32,128]{2,1,0:T(8,128)(2,1)S(1)}, u32[]{:S(2)}, u32[]{:S(2)}) %all-to-all-start.2) | async-done | bytes 65568 | tf_op jit(solution)/shard_map/cond/branch_1_fun/all_to_all | solution.py:26
  29.5 0.7 pivot_sum.32
  30.2 10.8 %all-to-all-start.3 = ((bf16[16,32,128]{2,1,0:T(8,128)(2,1)}), bf16[16,32,128]{2,1,0:T(8,128)(2,1)}, u32[]{:S(2)}, u32[]{:S(2)}) async-start(bf16[16,32,128]{2,1,0:T(8,128)(2,1)} %pivot_sum.32), calls=%async_computation.3 | async-start | bytes 262144 | tf_op jit(solution)/shard_map/cond/branch_1_fun/all_to_all | solution.py:26
  40.9 0.0 collective-permute-done.1
  40.9 9.3 %all-to-all-done.3 = bf16[16,32,128]{2,1,0:T(8,128)(2,1)} async-done(((bf16[16,32,128]{2,1,0:T(8,128)(2,1)}), bf16[16,32,128]{2,1,0:T(8,128)(2,1)}, u32[]{:S(2)}, u32[]{:S(2)}) %all-to-all-start.3) | async-done | bytes 131104 | tf_op jit(solution)/shard_map/cond/branch_1_fun/all_to_all | solution.py:26
  50.2 5.7 %first_half.1 = (f32[4,8,768]{2,1,0:T(8,128)S(1)}, f32[16,1,1152]{2,1,0:T(1,128)S(1)}, bf16[4,48,768]{2,1,0:T(8,128)(2,1)S(1)}, bf16[4,768,48]{2,1,0:T(8,128)(2,1)S(1)}, bf16[4,8,768]{2,1,0:T(8,128)(2,1)S(1)}) custom-call(s32[1]{0:T(128)} %bitcast.ahead_ref, bf16[4,40,768]{2,1,0:T(8,128)(2,1)S(1)} %all-to-all-done.62.row_ref, ...), custom_call_target="tpu_custom_call" | custom-call | flops 528482304 | bytes 623108 | tf_op jit(solution)/shard_map/first_half/pallas_call | solution.py:48
  55.9 10.4 %all_to_all.268.in_ref = f32[16,1,1152]{2,1,0:T(1,128)S(1)} all-to-all(f32[16,1,1152]{2,1,0:T(1,128)S(1)} %get-tuple-element.202), channel_id=1, replica_groups=mesh['y'=8,'zlo'=4,'core'=2,'zhi'=2,'x'=4] {'y','core'}, dimensions={0} | all-to-all | bytes 147456 | tf_op jit(solution)/shard_map/all_to_all | solution.py:26
  66.3 0.6 first_sum.1
  66.9 3.8 %all-to-all-start.64 = ((f32[8,1,1152]{2,1,0:T(1,128)}), f32[8,1,1152]{2,1,0:T(1,128)S(1)}, u32[]{:S(2)}, u32[]{:S(2)}) async-start(f32[8,1,1152]{2,1,0:T(1,128)} %first_sum.1), calls=%async_computation.64 | async-start | bytes 73728 | tf_op jit(solution)/shard_map/all_to_all | solution.py:26
  70.7 4.4 %second_half.1.sum_ref = f32[4,8,768]{2,1,0:T(8,128)S(1)} custom-call(s32[1]{0:T(128)} %bitcast.ahead_ref, bf16[4,48,768]{2,1,0:T(8,128)(2,1)S(1)} %get-tuple-element.198.row_all, bf16[4,768,48]{2,1,0:T(8,128)(2,1)S(1)} %get-tuple-element.199.col_all, bf16[4,8,768]{2,1,0:T(8,128)(2,1)S(1)} %get-tuple-element.200.col_probe, ...), custom_call_target="tpu_custom_call" | custom-call | flops 528482304 | bytes 737284 | tf_op jit(solution)/shard_map/second_half/pallas_call | solution.py:48
  75.1 2.2 %all-to-all-done.64.total_ref = f32[8,1,1152]{2,1,0:T(1,128)S(1)} async-done(((f32[8,1,1152]{2,1,0:T(1,128)}), f32[8,1,1152]{2,1,0:T(1,128)S(1)}, u32[]{:S(2)}, u32[]{:S(2)}) %all-to-all-start.64) | async-done | bytes 36896 | tf_op jit(solution)/shard_map/all_to_all | solution.py:26
  77.4 13.0 %all_to_all.269.in_ref = f32[4,8,1024]{2,1,0:T(8,128)S(1)} all-to-all(f32[4,8,1024]{2,1,0:T(8,128)S(1)} %join.1), channel_id=1, replica_groups=mesh['y'=8,'zlo'=4,'core'=2,'zhi'=2,'x'=4] {'x'}, dimensions={0} | all-to-all | bytes 262144 | tf_op jit(solution)/shard_map/all_to_all | solution.py:26
  90.3 0.6 finish.1
  (2 shorter events, 0.0 us)
Async XLA Ops:
  2.4 5.7 %copy-start = (bf16[4,40,768]{2,1,0:T(8,128)(2,1)S(1)}, bf16[4,40,768]{2,1,0:T(8,128)(2,1)}, u32[]{:S(2)}) copy-start(bf16[4,40,768]{2,1,0:T(8,128)(2,1)} %prepare.1.packed_ref) | copy-start | bytes 737284
  2.4 10.4 %all-to-all-start.62 = ((bf16[4,40,768]{2,1,0:T(8,128)(2,1)}), bf16[4,40,768]{2,1,0:T(8,128)(2,1)S(1)}, u32[]{:S(2)}, u32[]{:S(2)}) async-start(bf16[4,40,768]{2,1,0:T(8,128)(2,1)} %prepare.1.packed_ref), calls=%async_computation.62 | async-start | bytes 491520 | tf_op jit(solution)/shard_map/all_to_all | solution.py:26
  8.0 0.7 copy-start.1
  12.8 16.7 %all-to-all-start.2 = ((bf16[8,32,128]{2,1,0:T(8,128)(2,1)}), bf16[8,32,128]{2,1,0:T(8,128)(2,1)S(1)}, u32[]{:S(2)}, u32[]{:S(2)}) async-start(bf16[8,32,128]{2,1,0:T(8,128)(2,1)} %get-tuple-element.127), calls=%async_computation.2 | async-start | bytes 131072 | tf_op jit(solution)/shard_map/cond/branch_1_fun/all_to_all | solution.py:26
  22.9 18.1 %collective-permute-start.1 = (bf16[4,40,768]{2,1,0:T(8,128)(2,1)S(1)}, bf16[4,40,768]{2,1,0:T(8,128)(2,1)}, u32[]{:S(2)}, u32[]{:S(2)}) collective-permute-start(bf16[4,40,768]{2,1,0:T(8,128)(2,1)S(1)} %get-tuple-element.126), channel_id=1, source_target_pairs={{16,0},{497,1},{22,2},{503,3},{20,4},{501,5},{18,6},{499,7},{504,8... | collective-permute-start | bytes 737288 | tf_op jit(solution)/shard_map/cond/branch_1_fun/ppermute | solution.py:39
  30.2 20.0 %all-to-all-start.3 = ((bf16[16,32,128]{2,1,0:T(8,128)(2,1)}), bf16[16,32,128]{2,1,0:T(8,128)(2,1)}, u32[]{:S(2)}, u32[]{:S(2)}) async-start(bf16[16,32,128]{2,1,0:T(8,128)(2,1)} %pivot_sum.32), calls=%async_computation.3 | async-start | bytes 262144 | tf_op jit(solution)/shard_map/cond/branch_1_fun/all_to_all | solution.py:26
  66.9 10.4 %all-to-all-start.64 = ((f32[8,1,1152]{2,1,0:T(1,128)}), f32[8,1,1152]{2,1,0:T(1,128)S(1)}, u32[]{:S(2)}, u32[]{:S(2)}) async-start(f32[8,1,1152]{2,1,0:T(1,128)} %first_sum.1), calls=%async_computation.64 | async-start | bytes 73728 | tf_op jit(solution)/shard_map/all_to_all | solution.py:26

commit v8 on v7

--- a/solution.py
+++ b/solution.py
@@ -97,14 +97,15 @@
         out_ref[copy] = packed
 
 
-def own_pivots_kernel(first_ref, packed_ref, pivot_ref, out_ref):
+def own_pivots_kernel(first_ref, packed_ref, pivot_ref, out_ref, other_ref):
     count, rank = out_ref.shape[1:]
     points = packed_ref.shape[2]
     point = lax.broadcasted_iota(jnp.int32, (points, rank), 0) + first_ref[0]
     mask = jnp.where(point == pivot_ref[...], 1.0, 0.0).astype(jnp.bfloat16)
     part = jnp.dot(packed_ref[0, :count], mask, preferred_element_type=jnp.float32)
-    for copy in range(out_ref.shape[0]):
-        out_ref[copy] = part.astype(jnp.bfloat16)
+    for target in (out_ref, other_ref):
+        for copy in range(target.shape[0]):
+            target[copy] = part.astype(jnp.bfloat16)
 
 
 def sum_spread_kernel(in_ref, out_ref):
@@ -256,10 +257,13 @@
 
     first_point = (lax.axis_index(ALL_AXES) * row_count).astype(jnp.int32)
     pivot_row = pivots.reshape(1, rank)
-    pivot_part = local(
+    pivot_part, pivot_wide = local(
         own_pivots_kernel,
         "own_pivots",
-        shape((size_of(SECOND_SUM), count, rank), jnp.bfloat16),
+        (
+            shape((size_of(SECOND_SUM), count, rank), jnp.bfloat16),
+            shape((size_of(FIRST_SUM), count, rank), jnp.bfloat16),
+        ),
         first_point.reshape(1),
         packed,
         pivot_row,
@@ -269,20 +273,27 @@
     pivot_here = (pivot_row // row_count % width == lax.axis_index("x")).astype(jnp.int32)
 
     def fetch(shift):
-        def branch(data, part):
+        y_first = shift % 8 == 4 and shift < 16
+        one, two = (FIRST_SUM, SECOND_SUM) if y_first else (SECOND_SUM, FIRST_SUM)
+
+        def branch(data, part, wide):
             some = local(
                 sum_spread_kernel,
                 "pivot_sum",
-                shape((size_of(FIRST_SUM), count, rank), jnp.bfloat16),
-                exchanged(part, SECOND_SUM),
+                shape((size_of(two), count, rank), jnp.bfloat16),
+                exchanged(wide if y_first else part, one),
             )
             pieces = from_partner(data, shift)
-            return pieces, exchanged(some, FIRST_SUM)
+            some = exchanged(some, two)
+            if y_first:
+                spare = size_of(FIRST_SUM) - size_of(SECOND_SUM)
+                some = jnp.pad(some, ((0, spare), (0, 0), (0, 0)))
+            return pieces, some
 
         return branch
 
     pieces, pivot_all = lax.switch(
-        round_index[0] - 1, [fetch(k) for k in range(1, MAX_SHIFT + 1)], quad, pivot_part
+        round_index[0] - 1, [fetch(k) for k in range(1, MAX_SHIFT + 1)], quad, pivot_part, pivot_wide
     )
 
     product_scale = 8.0 / math.sqrt(block_points)

time: 92 us -> 93 us (1.011)
  the two profiles are of different devices: /device:TPU:1 before, /device:TPU:2 now
where the time goes in v8:
time: 93 us; the launch traced here: 91.4 us
  starting transfers between devices  31.6 us (34%)
  blocking collectives  24 us (26%)
  waiting for transfers between devices  19.1 us (21%)
  Pallas kernels  14.7 us (16%)
  between operations  1.35 us (1%)
    all_to_all x4, starting transfers between devices, exchanged(): return lax.all_to_all(x, axes, 0, 0)  25.9 us
    all_to_all x2, blocking collectives, exchanged(): return lax.all_to_all(x, axes, 0, 0)  24 us
    all_to_all x4, waiting for transfers between devices, exchanged(): return lax.all_to_all(x, axes, 0, 0)  19.1 us
    pallas_call x8, Pallas kernels, local(): pl.pallas_call(kernel, name=name, out_shape=out_shape, in_specs=specs, ou...  14.7 us
    ppermute x1, starting transfers between devices, from_partner(): return lax.ppermute(x, ALL_AXES, pairs)  5.72 us
  transfers between devices with their start and end apart: 5, of which 4 were waited for; matrix products, arithmetic and copies ran while one was open for 0% of the time, Pallas kernels for 7%

profile of v8, /device:TPU:2, one launch (start us, length us, event | category | flops | bytes accessed | tf_op | source)
XLA Modules:
  0.0 91.4 jit_solution(4543285506328970831)
XLA Ops:
  0.6 1.7 %prepare.1.packed_ref = bf16[4,40,768]{2,1,0:T(8,128)(2,1)} custom-call(f32[32,768]{1,0:T(8,128)} %feat_hbm.1, f32[1,32]{1,0:T(1,128)} %bitcast.8, bf16[8,768]{1,0:T(8,128)(2,1)} %probe_hbm.1), custom_call_target="tpu_custom_call" | custom-call | bytes 110720 | tf_op jit(solution)/shard_map/prepare/pallas_call | solution.py:48
  2.4 0.0 copy-start
  2.4 9.4 %all-to-all-start.62 = ((bf16[4,40,768]{2,1,0:T(8,128)(2,1)}), bf16[4,40,768]{2,1,0:T(8,128)(2,1)S(1)}, u32[]{:S(2)}, u32[]{:S(2)}) async-start(bf16[4,40,768]{2,1,0:T(8,128)(2,1)} %prepare.1.packed_ref), calls=%async_computation.62 | async-start | bytes 491520 | tf_op jit(solution)/shard_map/all_to_all | solution.py:26
  12.5 0.0 copy-start.1
  12.5 0.0 copy-done
  12.5 0.6 copy-done.1
  13.1 0.9 own_pivots.1
  14.0 2.9 %all-to-all-done.62.row_ref = bf16[4,40,768]{2,1,0:T(8,128)(2,1)S(1)} async-done(((bf16[4,40,768]{2,1,0:T(8,128)(2,1)}), bf16[4,40,768]{2,1,0:T(8,128)(2,1)S(1)}, u32[]{:S(2)}, u32[]{:S(2)}) %all-to-all-start.62) | async-done | bytes 245792 | tf_op jit(solution)/shard_map/all_to_all | solution.py:26
  16.9 32.5 %conditional.1 = (bf16[4,40,768]{2,1,0:T(8,128)(2,1)}, bf16[16,32,128]{2,1,0:T(8,128)(2,1)}) conditional(s32[]{:T(128)} %bitcast.2, (bf16[4,40,768]{2,1,0:T(8,128)(2,1)S(1)}, bf16[8,32,128]{2,1,0:T(8,128)(2,1)}) %tuple.131, (bf16[4,40,768]{2,1,0:T(8,128)(2,1)S(1)}, bf16[8,32,128]{2,1,0:T(8,128)(2,1)}) %tuple.131, ...), branch_computations={%region_0.1_spmd, %region_1.2_spmd, %region_2.3_spmd, %region_3.4_... | conditional | bytes 1835098 | solution.py:295
  16.9 5.9 %all-to-all-start.10 = ((bf16[8,32,128]{2,1,0:T(8,128)(2,1)}), bf16[8,32,128]{2,1,0:T(8,128)(2,1)S(1)}, u32[]{:S(2)}, u32[]{:S(2)}) async-start(bf16[8,32,128]{2,1,0:T(8,128)(2,1)} %get-tuple-element.135), calls=%async_computation.10 | async-start | bytes 131072 | tf_op jit(solution)/shard_map/cond/branch_5_fun/all_to_all | solution.py:26
  22.8 5.7 %collective-permute-start.5 = (bf16[4,40,768]{2,1,0:T(8,128)(2,1)S(1)}, bf16[4,40,768]{2,1,0:T(8,128)(2,1)}, u32[]{:S(2)}, u32[]{:S(2)}) collective-permute-start(bf16[4,40,768]{2,1,0:T(8,128)(2,1)S(1)} %get-tuple-element.134), channel_id=1, source_target_pairs={{48,0},{465,1},{54,2},{471,3},{52,4},{469,5},{50,6},{467,7},{472,8... | collective-permute-start | bytes 737288 | tf_op jit(solution)/shard_map/cond/branch_5_fun/ppermute | solution.py:39
  28.5 4.2 %all-to-all-done.10.in_ref = bf16[8,32,128]{2,1,0:T(8,128)(2,1)S(1)} async-done(((bf16[8,32,128]{2,1,0:T(8,128)(2,1)}), bf16[8,32,128]{2,1,0:T(8,128)(2,1)S(1)}, u32[]{:S(2)}, u32[]{:S(2)}) %all-to-all-start.10) | async-done | bytes 65568 | tf_op jit(solution)/shard_map/cond/branch_5_fun/all_to_all | solution.py:26
  32.7 0.7 pivot_sum.36
  33.4 7.3 %all-to-all-start.11 = ((bf16[16,32,128]{2,1,0:T(8,128)(2,1)}), bf16[16,32,128]{2,1,0:T(8,128)(2,1)}, u32[]{:S(2)}, u32[]{:S(2)}) async-start(bf16[16,32,128]{2,1,0:T(8,128)(2,1)} %pivot_sum.36), calls=%async_computation.11 | async-start | bytes 262144 | tf_op jit(solution)/shard_map/cond/branch_5_fun/all_to_all | solution.py:26
  40.7 0.0 collective-permute-done.5
  40.7 8.8 %all-to-all-done.11 = bf16[16,32,128]{2,1,0:T(8,128)(2,1)} async-done(((bf16[16,32,128]{2,1,0:T(8,128)(2,1)}), bf16[16,32,128]{2,1,0:T(8,128)(2,1)}, u32[]{:S(2)}, u32[]{:S(2)}) %all-to-all-start.11) | async-done | bytes 131104 | tf_op jit(solution)/shard_map/cond/branch_5_fun/all_to_all | solution.py:26
  49.5 5.7 %first_half.1 = (f32[4,8,768]{2,1,0:T(8,128)S(1)}, f32[16,1,1152]{2,1,0:T(1,128)S(1)}, bf16[4,48,768]{2,1,0:T(8,128)(2,1)S(1)}, bf16[4,768,48]{2,1,0:T(8,128)(2,1)S(1)}, bf16[4,8,768]{2,1,0:T(8,128)(2,1)S(1)}) custom-call(s32[1]{0:T(128)} %bitcast.ahead_ref, bf16[4,40,768]{2,1,0:T(8,128)(2,1)S(1)} %all-to-all-done.62.row_ref, ...), custom_call_target="tpu_custom_call" | custom-call | flops 528482304 | bytes 623108 | tf_op jit(solution)/shard_map/first_half/pallas_call | solution.py:48
  55.2 10.8 %all_to_all.270.in_ref = f32[16,1,1152]{2,1,0:T(1,128)S(1)} all-to-all(f32[16,1,1152]{2,1,0:T(1,128)S(1)} %get-tuple-element.206), channel_id=1, replica_groups=mesh['y'=8,'zlo'=4,'core'=2,'zhi'=2,'x'=4] {'y','core'}, dimensions={0} | all-to-all | bytes 147456 | tf_op jit(solution)/shard_map/all_to_all | solution.py:26
  66.0 0.6 first_sum.1
  66.6 3.3 %all-to-all-start.64 = ((f32[8,1,1152]{2,1,0:T(1,128)}), f32[8,1,1152]{2,1,0:T(1,128)S(1)}, u32[]{:S(2)}, u32[]{:S(2)}) async-start(f32[8,1,1152]{2,1,0:T(1,128)} %first_sum.1), calls=%async_computation.64 | async-start | bytes 73728 | tf_op jit(solution)/shard_map/all_to_all | solution.py:26
  70.0 4.4 %second_half.1.sum_ref = f32[4,8,768]{2,1,0:T(8,128)S(1)} custom-call(s32[1]{0:T(128)} %bitcast.ahead_ref, bf16[4,48,768]{2,1,0:T(8,128)(2,1)S(1)} %get-tuple-element.202.row_all, bf16[4,768,48]{2,1,0:T(8,128)(2,1)S(1)} %get-tuple-element.203.col_all, bf16[4,8,768]{2,1,0:T(8,128)(2,1)S(1)} %get-tuple-element.204.col_probe, ...), custom_call_target="tpu_custom_call" | custom-call | flops 528482304 | bytes 737284 | tf_op jit(solution)/shard_map/second_half/pallas_call | solution.py:48
  74.4 3.2 %all-to-all-done.64.total_ref = f32[8,1,1152]{2,1,0:T(1,128)S(1)} async-done(((f32[8,1,1152]{2,1,0:T(1,128)}), f32[8,1,1152]{2,1,0:T(1,128)S(1)}, u32[]{:S(2)}, u32[]{:S(2)}) %all-to-all-start.64) | async-done | bytes 36896 | tf_op jit(solution)/shard_map/all_to_all | solution.py:26
  77.6 13.2 %all_to_all.271.in_ref = f32[4,8,1024]{2,1,0:T(8,128)S(1)} all-to-all(f32[4,8,1024]{2,1,0:T(8,128)S(1)} %join.1), channel_id=1, replica_groups=mesh['y'=8,'zlo'=4,'core'=2,'zhi'=2,'x'=4] {'x'}, dimensions={0} | all-to-all | bytes 262144 | tf_op jit(solution)/shard_map/all_to_all | solution.py:26
  90.8 0.6 finish.1
  (2 shorter events, 0.0 us)
Async XLA Ops:
  2.4 10.1 %copy-start = (bf16[4,40,768]{2,1,0:T(8,128)(2,1)S(1)}, bf16[4,40,768]{2,1,0:T(8,128)(2,1)}, u32[]{:S(2)}) copy-start(bf16[4,40,768]{2,1,0:T(8,128)(2,1)} %prepare.1.packed_ref) | copy-start | bytes 737284
  2.4 14.6 %all-to-all-start.62 = ((bf16[4,40,768]{2,1,0:T(8,128)(2,1)}), bf16[4,40,768]{2,1,0:T(8,128)(2,1)S(1)}, u32[]{:S(2)}, u32[]{:S(2)}) async-start(bf16[4,40,768]{2,1,0:T(8,128)(2,1)} %prepare.1.packed_ref), calls=%async_computation.62 | async-start | bytes 491520 | tf_op jit(solution)/shard_map/all_to_all | solution.py:26
  12.5 0.7 copy-start.1
  16.9 15.8 %all-to-all-start.10 = ((bf16[8,32,128]{2,1,0:T(8,128)(2,1)}), bf16[8,32,128]{2,1,0:T(8,128)(2,1)S(1)}, u32[]{:S(2)}, u32[]{:S(2)}) async-start(bf16[8,32,128]{2,1,0:T(8,128)(2,1)} %get-tuple-element.135), calls=%async_computation.10 | async-start | bytes 131072 | tf_op jit(solution)/shard_map/cond/branch_5_fun/all_to_all | solution.py:26
  22.8 17.9 %collective-permute-start.5 = (bf16[4,40,768]{2,1,0:T(8,128)(2,1)S(1)}, bf16[4,40,768]{2,1,0:T(8,128)(2,1)}, u32[]{:S(2)}, u32[]{:S(2)}) collective-permute-start(bf16[4,40,768]{2,1,0:T(8,128)(2,1)S(1)} %get-tuple-element.134), channel_id=1, source_target_pairs={{48,0},{465,1},{54,2},{471,3},{52,4},{469,5},{50,6},{467,7},{472,8... | collective-permute-start | bytes 737288 | tf_op jit(solution)/shard_map/cond/branch_5_fun/ppermute | solution.py:39
  33.4 16.1 %all-to-all-start.11 = ((bf16[16,32,128]{2,1,0:T(8,128)(2,1)}), bf16[16,32,128]{2,1,0:T(8,128)(2,1)}, u32[]{:S(2)}, u32[]{:S(2)}) async-start(bf16[16,32,128]{2,1,0:T(8,128)(2,1)} %pivot_sum.36), calls=%async_computation.11 | async-start | bytes 262144 | tf_op jit(solution)/shard_map/cond/branch_5_fun/all_to_all | solution.py:26
  66.6 11.0 %all-to-all-start.64 = ((f32[8,1,1152]{2,1,0:T(1,128)}), f32[8,1,1152]{2,1,0:T(1,128)S(1)}, u32[]{:S(2)}, u32[]{:S(2)}) async-start(f32[8,1,1152]{2,1,0:T(1,128)} %first_sum.1), calls=%async_computation.64 | async-start | bytes 73728 | tf_op jit(solution)/shard_map/all_to_all | solution.py:26
